TPU v7x, 256 devices: a whole 4x4x8 slice. The times are simulated.
256 devices in a mesh: gx: 8 (over x, y_lo), gy: 8 (over z), gz: 4 (over y_hi, core).
Axes of the slice: x: 4, y: 4 (y_hi: 2, y_lo: 2; y = y_hi * 2 + y_lo), z: 8, core: 2. Of those that a mesh axis runs over, the one named last changes fastest.
Arguments:
- tokens: bfloat16 [32, 64, 64, 256], P('gx', 'gy', 'gz'), may hold values from -6 to 6
- cotangent: bfloat16 [16, 32, 32, 512], P('gx', 'gy', 'gz'), may hold values from -6 to 6
- gain_attn: float32 [256], replicated, may hold values from 0.1 to 1.9
- w_qkv: bfloat16 [256, 768], replicated, may hold values from -1 to 1
- w_proj: bfloat16 [256, 256], replicated, may hold values from -0.375 to 0.375
- gain_merge: float32 [2048], replicated, may hold values from 0.1 to 1.9
- w_merge: bfloat16 [2048, 512], replicated, may hold values from -0.125 to 0.125
Outputs:
- merged: bfloat16 [16, 32, 32, 512], P('gx', 'gy', 'gz')
- d_tokens: bfloat16 [32, 64, 64, 256], P('gx', 'gy', 'gz')
- d_gain_attn: float32 [256], replicated
- d_qkv: bfloat16 [256, 768], replicated
- d_proj: bfloat16 [256, 256], replicated
- d_gain_merge: float32 [2048], replicated
- d_merge: bfloat16 [2048, 512], replicated
All inputs are finite; a program needn't handle non-finite values.
Results may differ from a plain program's by a relative error of at most 0.014.
The roundings to bfloat16 on the way count: a program that leaves them out, or rounds other values in their place, can miss the bound.
Values may be sent and summed in bfloat16 or wider, within the bound.
A program may use at most 64 MiB of HBM per device.

v0:
```python
import jax
import jax.numpy as jnp
from jax import lax
from jax.sharding import PartitionSpec as P

HEADS = 8
WINDOW = 4


epsilon = 1e-05


def shifted(block, axis, distance):
    devices = range(lax.axis_size(axis))
    route = [((i - distance) % len(devices), i) for i in devices]
    return lax.ppermute(block, axis, route)


def normed(values, scaling):
    average = jnp.mean(values, axis=-1, keepdims=True)
    centred = values - average
    variance = jnp.mean(centred * centred, axis=-1, keepdims=True)
    return centred * lax.rsqrt(variance + epsilon) * scaling


def to_windows(volume, window_side):
    extent_a, extent_b, extent_c, features = volume.shape
    shaped = volume.reshape(
        extent_a // window_side,
        window_side,
        extent_b // window_side,
        window_side,
        extent_c // window_side,
        window_side,
        features,
    )
    return shaped.transpose(0, 2, 4, 1, 3, 5, 6).reshape(
        -1, window_side * window_side * window_side, features
    )


def from_windows(windows, extent_a, extent_b, extent_c, window_side):
    features = windows.shape[-1]
    shaped = windows.reshape(
        extent_a // window_side,
        extent_b // window_side,
        extent_c // window_side,
        window_side,
        window_side,
        window_side,
        features,
    )
    return shaped.transpose(0, 3, 1, 4, 2, 5, 6).reshape(extent_a, extent_b, extent_c, features)


def group_pairs(volume):
    extent_a, extent_b, extent_c, features = volume.shape
    shaped = volume.reshape(extent_a // 2, 2, extent_b // 2, 2, extent_c // 2, 2, features)
    return shaped.transpose(0, 2, 4, 1, 3, 5, 6).reshape(
        extent_a // 2, extent_b // 2, extent_c // 2, 8 * features
    )


def split_pairs(grouped, features):
    extent_a, extent_b, extent_c = grouped.shape[:3]
    shaped = grouped.reshape(extent_a, extent_b, extent_c, 2, 2, 2, features)
    return shaped.transpose(0, 3, 1, 4, 2, 5, 6).reshape(
        2 * extent_a, 2 * extent_b, 2 * extent_c, features
    )


def inner_rows(left_rows, right_rows):
    return lax.dot_general(
        left_rows, right_rows, (((0,), (0,)), ((), ())), preferred_element_type=jnp.float32
    )


def times_t(left_rows, matrix):
    return lax.dot_general(
        left_rows, matrix, (((1,), (1,)), ((), ())), preferred_element_type=jnp.float32
    )


def batched(form, left_side, right_side):
    return jnp.einsum(form, left_side, right_side, preferred_element_type=jnp.float32)


def move_faces(volume, depth_cells, forward):
    direction = -1 if forward else 1
    leading = volume[:depth_cells] if forward else volume[-depth_cells:]
    arrived = shifted(leading, "gx", direction)
    volume = (
        jnp.concatenate([volume[depth_cells:], arrived], 0)
        if forward
        else jnp.concatenate([arrived, volume[:-depth_cells]], 0)
    )
    leading = volume[:, :depth_cells] if forward else volume[:, -depth_cells:]
    arrived = shifted(leading, "gy", direction)
    volume = (
        jnp.concatenate([volume[:, depth_cells:], arrived], 1)
        if forward
        else jnp.concatenate([arrived, volume[:, :-depth_cells]], 1)
    )
    leading = volume[:, :, :depth_cells] if forward else volume[:, :, -depth_cells:]
    arrived = shifted(leading, "gz", direction)
    volume = (
        jnp.concatenate([volume[:, :, depth_cells:], arrived], 2)
        if forward
        else jnp.concatenate([arrived, volume[:, :, :-depth_cells]], 2)
    )
    return volume


def attend_forward(rolled, gain_attn, w_qkv, w_proj, head_count):
    extent_a, extent_b, extent_c, channels = rolled.shape
    windows = to_windows(rolled, WINDOW)
    windows_count, window_cells = (windows.shape[0], windows.shape[1])
    flat_rows = windows.reshape(-1, channels).astype(jnp.float32)
    normal_rows = normed(flat_rows, gain_attn).astype(jnp.bfloat16)
    project = jnp.dot(normal_rows, w_qkv, preferred_element_type=jnp.float32).astype(jnp.bfloat16)
    project = project.reshape(windows_count, window_cells, 3, head_count, channels // head_count)
    queries = project[:, :, 0]
    keys_all = project[:, :, 1]
    values_all = project[:, :, 2]
    factor = (channels // head_count) ** (-0.5)
    scores = batched("wqhd,wkhd->whqk", queries, keys_all) * factor
    weights = jax.nn.softmax(scores, axis=-1)
    rounded = weights.astype(jnp.bfloat16)
    mixed_rows = (
        batched("whqk,wkhd->wqhd", rounded, values_all).astype(jnp.bfloat16).reshape(-1, channels)
    )
    output = jnp.dot(mixed_rows, w_proj, preferred_element_type=jnp.float32)
    summed_rows = (flat_rows + output).astype(jnp.bfloat16)
    result = from_windows(
        summed_rows.reshape(windows_count, window_cells, channels),
        extent_a,
        extent_b,
        extent_c,
        WINDOW,
    )
    saved_state = (
        flat_rows,
        normal_rows,
        queries,
        keys_all,
        values_all,
        weights,
        rounded,
        mixed_rows,
    )
    return (result, saved_state)


def attend_backward(saved_state, grad_sum, gain_attn, w_qkv, w_proj, head_count):
    flat_rows, normal_rows, queries, keys_all, values_all, weights, rounded, mixed_rows = (
        saved_state
    )
    windows_count, window_cells = (queries.shape[0], queries.shape[1])
    extent_a, extent_b, extent_c, channels = grad_sum.shape
    factor = (channels // head_count) ** (-0.5)
    grad_rows = to_windows(grad_sum, WINDOW).reshape(-1, channels)
    grad_proj = inner_rows(mixed_rows, grad_rows)
    grad_mixed = times_t(grad_rows, w_proj).astype(jnp.bfloat16)
    grad_mixed = grad_mixed.reshape(windows_count, window_cells, head_count, channels // head_count)
    grad_weights = batched("wqhd,wkhd->whqk", grad_mixed, values_all)
    grad_values = batched("whqk,wqhd->wkhd", rounded, grad_mixed)
    grad_scores = weights * (grad_weights - jnp.sum(grad_weights * weights, axis=-1, keepdims=True))
    grad_scaled = (grad_scores * factor).astype(jnp.bfloat16)
    grad_queries = batched("whqk,wkhd->wqhd", grad_scaled, keys_all)
    grad_keys = batched("whqk,wqhd->wkhd", grad_scaled, queries)
    grad_project = (
        jnp.stack([grad_queries, grad_keys, grad_values], axis=2)
        .astype(jnp.bfloat16)
        .reshape(-1, 3 * channels)
    )
    grad_qkv = inner_rows(normal_rows, grad_project)
    grad_normal = times_t(grad_project, w_qkv)
    ignored, pullback = jax.vjp(normed, flat_rows, gain_attn)
    grad_flat, grad_gain = pullback(grad_normal)
    grad_total = (grad_rows.astype(jnp.float32) + grad_flat).astype(jnp.bfloat16)
    result = from_windows(
        grad_total.reshape(windows_count, window_cells, channels),
        extent_a,
        extent_b,
        extent_c,
        WINDOW,
    )
    return (result, grad_gain, grad_qkv, grad_proj)


def merge_pass(volume, gain_merge, w_merge, grad_out):
    channels = volume.shape[-1]
    grouped = group_pairs(volume)
    flat_rows = grouped.reshape(-1, grouped.shape[-1]).astype(jnp.float32)
    normal_rows = normed(flat_rows, gain_merge).astype(jnp.bfloat16)
    output = jnp.dot(normal_rows, w_merge, preferred_element_type=jnp.float32).astype(jnp.bfloat16)
    output = output.reshape(grouped.shape[:3] + (w_merge.shape[1],))
    grad_rows = grad_out.reshape(-1, grad_out.shape[-1])
    grad_weight = inner_rows(normal_rows, grad_rows)
    grad_normal = times_t(grad_rows, w_merge)
    ignored, pullback = jax.vjp(normed, flat_rows, gain_merge)
    grad_flat, grad_gain = pullback(grad_normal)
    grad_volume = split_pairs(grad_flat.astype(jnp.bfloat16).reshape(grouped.shape), channels)
    return (output, grad_volume, grad_gain, grad_weight)


def local(tokens, cotangent, gain_attn, w_qkv, w_proj, gain_merge, w_merge):
    half_window = WINDOW // 2
    rolled = move_faces(tokens, half_window, True)
    summed, saved_state = attend_forward(rolled, gain_attn, w_qkv, w_proj, HEADS)
    natural = move_faces(summed, half_window, False)
    merged, grad_natural, grad_gm, grad_wm = merge_pass(natural, gain_merge, w_merge, cotangent)
    grad_sum = move_faces(grad_natural, half_window, True)
    grad_rolled, grad_ga, grad_wq, grad_wp = attend_backward(
        saved_state, grad_sum, gain_attn, w_qkv, w_proj, HEADS
    )
    d_tokens = move_faces(grad_rolled, half_window, False)
    device_count = lax.axis_size("gx") * lax.axis_size("gy") * lax.axis_size("gz")
    total_tokens = tokens.shape[0] * tokens.shape[1] * tokens.shape[2] * device_count
    token_scale = float(total_tokens) ** (-0.5)
    merge_scale = float(total_tokens // 8) ** (-0.5)
    totals = lax.psum((grad_ga, grad_wq, grad_wp, grad_gm, grad_wm), ("gx", "gy", "gz"))
    return (
        merged,
        d_tokens,
        totals[0] * token_scale,
        (totals[1] * token_scale).astype(jnp.bfloat16),
        (totals[2] * token_scale).astype(jnp.bfloat16),
        totals[3] * merge_scale,
        (totals[4] * merge_scale).astype(jnp.bfloat16),
    )


def solution(mesh):
    return jax.shard_map(
        local,
        mesh=mesh,
        in_specs=(P("gx", "gy", "gz", None), P("gx", "gy", "gz", None), P(), P(), P(), P(), P()),
        out_specs=(P("gx", "gy", "gz", None), P("gx", "gy", "gz", None), P(), P(), P(), P(), P()),
        check_vma=False,
    )
```

profile of v0, /device:TPU:1, one launch (start us, length us, event | category | flops | bytes accessed | tf_op | source)
XLA Modules:
  0.0 404.5 jit_solution(2705616639397737380)
XLA Ops:
  7.2 1.1 fusion.55
  8.4 4.4 %collective-permute-start = (bf16[2,8,16,256]{3,2,1,0:T(8,128)(2,1)S(1)}, bf16[2,8,16,256]{3,2,1,0:T(8,128)(2,1)S(1)}, u32[]{:S(2)}, u32[]{:S(2)}) collective-permute-start(bf16[2,8,16,256]{3,2,1,0:T(8,128)(2,1)S(1)} %get-tuple-element.30), channel_id=1, source_target_pairs={{32,0},{64,32},{96,64},{128,96},{160,128},{192,160},{224,192},{0,2... | collective-permute-start | bytes 393224 | tf_op jit(solution)/shard_map/ppermute | solution.py:16
  12.8 2.2 collective-permute-done
  14.9 5.6 %collective-permute-start.1 = (bf16[4,2,16,256]{3,2,1,0:T(8,128)(2,1)S(1)}, bf16[4,2,16,256]{3,2,1,0:T(8,128)(2,1)S(1)}, u32[]{:S(2)}, u32[]{:S(2)}) collective-permute-start(bf16[4,2,16,256]{3,2,1,0:T(8,128)(2,1)S(1)} %pad_maximum_fusion.4), channel_id=1, source_target_pairs={{4,0},{8,4},{12,8},{16,12},{20,16},{24,20},{28,24},{0,28},{5,1},{9... | collective-permute-start | bytes 196616 | tf_op jit(solution)/shard_map/ppermute | solution.py:16
  20.6 1.3 collective-permute-done.1
  21.9 2.5 collective-permute-start.2
  24.5 4.0 collective-permute-done.2
  29.2 0.4 multiply_reduce_fusion.7
  29.6 0.9 copy.138
  30.7 0.6 copy-done.14
  31.2 1.2 reshape.204
  32.5 2.5 convolution_convert_fusion
  35.0 2.3 copy.70
  37.3 3.2 reshape.198
  40.5 2.5 fusion.51
  43.1 3.5 fusion.56
  46.6 2.2 fusion.18
  48.7 1.1 copy.75
  49.9 1.4 reshape.199
  51.3 1.9 fusion.19
  53.2 1.0 reshape_reshape.14
  54.9 5.8 %collective-permute-done.3 = bf16[2,8,16,256]{3,2,1,0:T(8,128)(2,1)S(1)} collective-permute-done((bf16[2,8,16,256]{3,2,1,0:T(8,128)(2,1)S(1)}, bf16[2,8,16,256]{3,2,1,0:T(8,128)(2,1)S(1)}, u32[]{:S(2)}, u32[]{:S(2)}) %collective-permute-start.3) | collective-permute-done | bytes 131104 | tf_op jit(solution)/shard_map/ppermute | solution.py:16
  60.7 0.6 slice.141
  61.4 5.1 %collective-permute-done.4 = bf16[4,2,16,256]{3,2,1,0:T(8,128)(2,1)S(1)} collective-permute-done((bf16[4,2,16,256]{3,2,1,0:T(8,128)(2,1)}, bf16[4,2,16,256]{3,2,1,0:T(8,128)(2,1)S(1)}, u32[]{:S(2)}, u32[]{:S(2)}) %collective-permute-start.4) | collective-permute-done | bytes 65568 | tf_op jit(solution)/shard_map/ppermute | solution.py:16
  66.5 0.7 pad_maximum_fusion.7
  67.2 3.6 collective-permute-start.5
  70.8 1.0 multiply_convert_fusion.4
  71.8 0.8 convert_element_type.136
  72.6 0.8 fusion.31
  74.1 0.5 multiply_reduce_fusion.6
  75.3 0.9 convert_element_type.140
  76.2 0.9 multiply_reduce_fusion.2
  78.0 1.2 collective-permute-start.6
  79.2 2.7 fusion.59
  81.9 1.3 collective-permute-done.6
  83.3 1.4 collective-permute-start.7
  85.0 1.5 collective-permute-done.7
  86.6 2.2 collective-permute-start.8
  88.9 3.9 collective-permute-done.8
  93.1 0.9 fusion.58
  94.3 0.8 copy.82
  95.2 1.3 reshape.203
  96.5 3.1 convolution_bitcast_fusion
  99.6 1.8 fusion.25
  101.4 5.3 %fusion.12 = bf16[8,64,1,8,32]{1,4,3,0,2:T(8,128)(2,1)} fusion(f32[8,8,64,64]{2,3,1,0:T(8,128)} %fusion.25, bf16[8,64,1,8,32]{1,0,4,3,2:T(8,128)(2,1)} %get-tuple-element.20, f32[8,8,64,64]{2,3,1,0:T(8,128)} %get-tuple-element.36, f32[8,8,64]{2,1,0:T(8,128)S(1)} %copy-done.23), kind=kOutput, calls=%fused_computation.13 | convolution fusion | flops 18616384 | bytes 2637824 | tf_op jit(solution)/shard_map/whqk,wkhd->wqhd/dot_general | solution.py:85
  106.7 5.1 %fusion.15 = bf16[8,64,1,8,32]{1,4,3,0,2:T(8,128)(2,1)} fusion(f32[8,8,64,64]{2,3,1,0:T(8,128)} %fusion.25, bf16[8,64,1,8,32]{1,0,4,3,2:T(8,128)(2,1)S(1)} %copy-done.7, f32[8,8,64,64]{2,3,1,0:T(8,128)} %get-tuple-element.36, f32[8,8,64]{2,1,0:T(8,128)S(1)} %copy-done.23), kind=kOutput, calls=%fused_computation.14 | convolution fusion | flops 18616384 | bytes 2637824 | tf_op jit(solution)/shard_map/whqk,wqhd->wkhd/dot_general | solution.py:85
  111.7 1.7 maximum_convert_fusion
  113.5 2.2 copy.88
  115.6 3.4 convert_element_type.133
  119.1 2.4 fusion.57
  121.6 1.0 copy-done.2
  122.6 1.8 multiply_reduce_fusion.3
  125.3 1.2 convolution_convert_fusion.3
  126.5 77.4 %all-reduce = (f32[256]{0:T(256)S(1)}, f32[2048]{0:T(1024)S(1)}) all-reduce(f32[256]{0:T(256)S(1)} %get-tuple-element.7, f32[2048]{0:T(1024)S(1)} %get-tuple-element.9), channel_id=1, replica_groups=mesh['gx'=8,'gy'=8,'gz'=4] {'gx','gy','gz'}, use_global_device_ids=true, to_apply=%region_12.0 | all-reduce | flops 2304 | bytes 18432 | tf_op jit(solution)/shard_map/psum | solution.py:222
  204.1 0.6 broadcast_multiply_fusion.1
  204.7 4.0 collective-permute-done.10
  208.7 2.6 collective-permute-start.11
  211.3 0.6 broadcast_multiply_fusion.3
  211.9 0.5 collective-permute-done.11
  212.3 0.8 fusion.29
  213.1 176.9 %all-reduce.4.cloned.1.call-done = (f32[256,768]{1,0:T(8,128)}, f32[256,256]{1,0:T(8,128)}, f32[2048,512]{1,0:T(8,128)}) async-done(((f32[256,768]{1,0:T(8,128)}, f32[256,256]{1,0:T(8,128)}, f32[2048,512]{1,0:T(8,128)}), (f32[256,768]{1,0:T(8,128)}, f32[256,256]{1,0:T(8,128)}, f32[2048,512]{1,0:T(8,128)})) %all-reduce.4.cloned.1.call-update) | async-done | bytes 5242896 | tf_op jit(solution)/shard_map/psum | solution.py:222
  390.0 1.9 multiply_convert_fusion.2
  391.9 1.6 multiply_convert_fusion.9
  393.5 4.1 %multiply_convert_fusion = bf16[2048,512]{1,0:T(8,128)(2,1)} fusion(f32[2048,512]{1,0:T(8,128)} %get-tuple-element.15), kind=kLoop, calls=%fused_computation.2 | loop fusion | flops 2097152 | bytes 6291456 | tf_op jit(solution)/shard_map/convert_element_type | solution.py:230
  (112 shorter events, 6.2 us)
Async XLA Ops:
  7.2 69.0 %copy-start = (bf16[2048,512]{1,0:T(8,128)(2,1)S(1)}, bf16[2048,512]{1,0:T(8,128)(2,1)}, u32[]{:S(2)}) copy-start(bf16[2048,512]{1,0:T(8,128)(2,1)} %param.13) | copy-start | bytes 6291460
  7.2 382.8 %all-reduce.4.cloned.1.call-start = ((), (), s32[]{:S(2)}) async-start(), calls=%async_computation | async-start | bytes 10485760 | tf_op jit(solution)/shard_map/psum | solution.py:222
  8.4 6.6 %collective-permute-start = (bf16[2,8,16,256]{3,2,1,0:T(8,128)(2,1)S(1)}, bf16[2,8,16,256]{3,2,1,0:T(8,128)(2,1)S(1)}, u32[]{:S(2)}, u32[]{:S(2)}) collective-permute-start(bf16[2,8,16,256]{3,2,1,0:T(8,128)(2,1)S(1)} %get-tuple-element.30), channel_id=1, source_target_pairs={{32,0},{64,32},{96,64},{128,96},{160,128},{192,160},{224,192},{0,2... | collective-permute-start | bytes 393224 | tf_op jit(solution)/shard_map/ppermute | solution.py:16
  14.9 7.0 %collective-permute-start.1 = (bf16[4,2,16,256]{3,2,1,0:T(8,128)(2,1)S(1)}, bf16[4,2,16,256]{3,2,1,0:T(8,128)(2,1)S(1)}, u32[]{:S(2)}, u32[]{:S(2)}) collective-permute-start(bf16[4,2,16,256]{3,2,1,0:T(8,128)(2,1)S(1)} %pad_maximum_fusion.4), channel_id=1, source_target_pairs={{4,0},{8,4},{12,8},{16,12},{20,16},{24,20},{28,24},{0,28},{5,1},{9... | collective-permute-start | bytes 196616 | tf_op jit(solution)/shard_map/ppermute | solution.py:16
  21.9 6.6 %collective-permute-start.2 = (bf16[4,8,2,256]{3,2,1,0:T(2,128)(2,1)S(1)}, bf16[4,8,2,256]{3,2,1,0:T(2,128)(2,1)S(1)}, u32[]{:S(2)}, u32[]{:S(2)}) collective-permute-start(bf16[4,8,2,256]{3,2,1,0:T(2,128)(2,1)S(1)} %pad_maximum_fusion.8), channel_id=1, source_target_pairs={{1,0},{2,1},{3,2},{0,3},{5,4},{6,5},{7,6},{4,7},{9,8},{10,9},{11,1... | collective-permute-start | bytes 98312 | tf_op jit(solution)/shard_map/ppermute | solution.py:16
  28.8 3.7 copy-start.16
  29.2 5.8 %copy-start.10 = (f32[512]{0:T(512)}, f32[512]{0:T(512)S(1)}, u32[]{:S(2)}) copy-start(f32[512]{0:T(512)S(1)} %div.53) | copy-start | bytes 6148
  30.7 0.6 copy-start.14
  31.2 6.1 %copy-start.12 = (f32[512]{0:T(512)}, f32[512]{0:T(512)S(1)}, u32[]{:S(2)}) copy-start(f32[512]{0:T(512)S(1)} %rsqrt.28) | copy-start | bytes 6148
  32.5 18.8 %copy-start.1 = (f32[512,256]{1,0:T(8,128)}, f32[512,256]{1,0:T(8,128)S(1)}, u32[]{:S(2)}) copy-start(f32[512,256]{1,0:T(8,128)S(1)} %reshape.204) | copy-start | bytes 1572868
  46.6 2.2 copy-start.22
  49.9 11.5 %copy-start.9 = (f32[2048]{0:T(1024)S(1)}, f32[2048]{0:T(1024)}, u32[]{:S(2)}) copy-start(f32[2048]{0:T(1024)} %param.12) | copy-start | bytes 24580
  54.6 6.1 %collective-permute-start.3 = (bf16[2,8,16,256]{3,2,1,0:T(8,128)(2,1)S(1)}, bf16[2,8,16,256]{3,2,1,0:T(8,128)(2,1)S(1)}, u32[]{:S(2)}, u32[]{:S(2)}) collective-permute-start(bf16[2,8,16,256]{3,2,1,0:T(8,128)(2,1)S(1)} %copy.77), channel_id=1, source_target_pairs={{224,0},{0,32},{32,64},{64,96},{96,128},{128,160},{160,192},{192,2... | collective-permute-start | bytes 393224 | tf_op jit(solution)/shard_map/ppermute | solution.py:16
  61.4 5.2 %collective-permute-start.4 = (bf16[4,2,16,256]{3,2,1,0:T(8,128)(2,1)}, bf16[4,2,16,256]{3,2,1,0:T(8,128)(2,1)S(1)}, u32[]{:S(2)}, u32[]{:S(2)}) collective-permute-start(bf16[4,2,16,256]{3,2,1,0:T(8,128)(2,1)} %slice.141), channel_id=1, source_target_pairs={{28,0},{0,4},{4,8},{8,12},{12,16},{16,20},{20,24},{24,28},{29,1},{... | collective-permute-start | bytes 196616 | tf_op jit(solution)/shard_map/ppermute | solution.py:16
  67.2 5.4 %collective-permute-start.5 = (bf16[4,8,2,256]{3,2,1,0:T(2,128)(2,1)}, bf16[4,8,2,256]{3,2,1,0:T(2,128)(2,1)}, u32[]{:S(2)}, u32[]{:S(2)}) collective-permute-start(bf16[4,8,2,256]{3,2,1,0:T(2,128)(2,1)} %pad_maximum_fusion.7), channel_id=1, source_target_pairs={{3,0},{0,1},{1,2},{2,3},{7,4},{4,5},{5,6},{6,7},{11,8},{8,9},{9,10... | collective-permute-start | bytes 98312 | tf_op jit(solution)/shard_map/ppermute | solution.py:16
  73.7 2.5 copy-start.8
  74.1 3.0 copy-start.18
  74.7 2.5 copy-start.20
  77.1 2.1 copy-start.5
  78.0 5.2 %collective-permute-start.6 = (bf16[2,8,16,256]{3,0,2,1:T(2,128)(2,1)S(1)}, bf16[2,8,16,256]{3,0,2,1:T(2,128)(2,1)S(1)}, u32[]{:S(2)}, u32[]{:S(2)}) collective-permute-start(bf16[2,8,16,256]{3,0,2,1:T(2,128)(2,1)S(1)} %bitcast.121), channel_id=1, source_target_pairs={{32,0},{64,32},{96,64},{128,96},{160,128},{192,160},{224,192},{0,2... | collective-permute-start | bytes 393224 | tf_op jit(solution)/shard_map/ppermute | solution.py:16
  81.9 12.2 %copy-start.6 = (bf16[256,256]{1,0:T(8,128)(2,1)S(1)}, bf16[256,256]{1,0:T(8,128)(2,1)}, u32[]{:S(2)}) copy-start(bf16[256,256]{1,0:T(8,128)(2,1)} %param.11) | copy-start | bytes 393220
  83.3 3.2 collective-permute-start.7
  86.6 6.2 %collective-permute-start.8 = (bf16[4,8,2,256]{3,0,2,1:T(4,128)(2,1)S(1)}, bf16[4,8,2,256]{3,0,2,1:T(4,128)(2,1)S(1)}, u32[]{:S(2)}, u32[]{:S(2)}) collective-permute-start(bf16[4,8,2,256]{3,0,2,1:T(4,128)(2,1)S(1)} %pad_maximum_fusion.6), channel_id=1, source_target_pairs={{1,0},{2,1},{3,2},{0,3},{5,4},{6,5},{7,6},{4,7},{9,8},{10,9},{11,1... | collective-permute-start | bytes 98312 | tf_op jit(solution)/shard_map/ppermute | solution.py:16
  96.4 3.1 copy-start.3
  99.6 1.8 copy-start.23
  101.4 5.3 %copy-start.7 = (bf16[8,64,1,8,32]{1,0,4,3,2:T(8,128)(2,1)S(1)}, bf16[8,64,1,8,32]{1,0,4,3,2:T(8,128)(2,1)}, u32[]{:S(2)}) copy-start(bf16[8,64,1,8,32]{1,0,4,3,2:T(8,128)(2,1)} %get-tuple-element.21) | copy-start | bytes 786436
  113.5 5.6 %copy-start.4 = (bf16[512,256]{1,0:T(8,128)(2,1)S(1)}, bf16[512,256]{1,0:T(8,128)(2,1)}, u32[]{:S(2)}) copy-start(bf16[512,256]{1,0:T(8,128)(2,1)} %convert_element_type.136) | copy-start | bytes 786436
  121.5 1.0 copy-start.2
  121.5 1.0 copy-start.11
  121.5 1.0 copy-start.13
  121.5 1.0 copy-start.17
  122.6 1.8 copy-start.15
  124.4 0.9 copy-start.19
  124.4 0.9 copy-start.21
  125.2 78.8 %collective-permute-start.9 = (bf16[2,8,16,256]{3,2,1,0:T(8,128)(2,1)S(1)}, bf16[2,8,16,256]{3,2,1,0:T(8,128)(2,1)S(1)}, u32[]{:S(2)}, u32[]{:S(2)}) collective-permute-start(bf16[2,8,16,256]{3,2,1,0:T(8,128)(2,1)S(1)} %slice.125), channel_id=1, source_target_pairs={{224,0},{0,32},{32,64},{64,96},{96,128},{128,160},{160,192},{192,2... | collective-permute-start | bytes 393224 | tf_op jit(solution)/shard_map/ppermute | solution.py:16
  204.0 4.7 %collective-permute-start.10 = (bf16[4,2,16,256]{3,2,1,0:T(8,128)(2,1)S(1)}, bf16[4,2,16,256]{3,2,1,0:T(8,128)(2,1)S(1)}, u32[]{:S(2)}, u32[]{:S(2)}) collective-permute-start(bf16[4,2,16,256]{3,2,1,0:T(8,128)(2,1)S(1)} %slice.151), channel_id=1, source_target_pairs={{28,0},{0,4},{4,8},{8,12},{12,16},{16,20},{20,24},{24,28},{29,1},{... | collective-permute-start | bytes 196616 | tf_op jit(solution)/shard_map/ppermute | solution.py:16
  208.7 3.6 collective-permute-start.11
Sparse Core Ops, SparseCore 0:
  121.7 268.2 all-reduce.3
where the time goes:
time: 406 us; the launch traced here: 404 us
  waiting for transfers between devices  206 us (51%)
  blocking collectives  77.4 us (19%)
  matrix products  35.4 us (9%)
  local copies, waits for them, and re-layouts  29 us (7%)
  starting transfers between devices  24.1 us (6%)
  other arithmetic  17.5 us (4%)
  between operations  14.6 us (4%)
    psum x1, waiting for transfers between devices, local(): lax.psum((grad_ga, grad_wq, grad_wp, grad_gm, grad_wm), ('gx', 'gy', 'gz'))  177 us
    psum x1, blocking collectives, local(): lax.psum((grad_ga, grad_wq, grad_wp, grad_gm, grad_wm), ('gx', 'gy', 'gz'))  77.4 us
    ppermute x12, waiting for transfers between devices, shifted(): return lax.ppermute(block, axis, route)  29.6 us
    ppermute x12, starting transfers between devices, shifted(): return lax.ppermute(block, axis, route)  24.1 us
    dot_general x5, matrix products, batched(): jnp.einsum(form, left_side, right_side, preferred_element_type=jnp.float32)  17.4 us
  transfers between devices with their start and end apart: 13, of which 11 were waited for; matrix products, arithmetic and copies ran while one was open for 3% of the time, Pallas kernels for 0%

commit v1 on v0

v1 whole, which is shorter than its diff:
```python
import functools

import jax
import jax.numpy as jnp
import numpy as np
from jax import lax
from jax.experimental import pallas as pl
from jax.experimental.pallas import tpu as pltpu
from jax.sharding import PartitionSpec as P

MESH = pl.DeviceIdType.MESH
HEADS = 8
WIDTH = 256
CELLS = 512
GROUPS = 64
ROWS = CELLS + 2 * GROUPS
FACTOR = 32 ** -0.5
EPSILON = 1e-05
TOKENS = 131072
TOKEN_SCALE = float(TOKENS) ** (-0.5)
MERGE_SCALE = float(TOKENS // 8) ** (-0.5)
BF16, F32 = jnp.bfloat16, jnp.float32

KINDS = [(a, b, c) for a in (0, 1) for b in (0, 1) for c in (0, 1)]


def kind_groups(kind):
    a, b, c = kind
    return [
        (i, j, k)
        for i in ([0] if a else [1])
        for j in ([0] if b else [1, 2, 3])
        for k in ([0] if c else list(range(1, 8)))
    ]


SIZES = [-(-10 * len(kind_groups(kind)) // 16) * 16 for kind in KINDS]
STARTS = [sum(SIZES[:i]) for i in range(8)]
HALO = sum(SIZES)


def orderings():
    leave, enter = np.zeros((HALO, ROWS), np.float32), np.zeros((ROWS, HALO), np.float32)
    for kind, start in zip(KINDS, STARTS):
        for at, (i, j, k) in enumerate(kind_groups(kind)):
            si, sj, sk = (i - 1) % 2, (j - 1) % 4, (k - 1) % 8
            window, place = (sj // 2) * 4 + sk // 2, si * 4 + (sj % 2) * 2 + sk % 2
            for o in range(8):
                cell = ((2 * i + o // 4) * 8 + 2 * j + o // 2 % 2) * 16 + 2 * k + o % 2
                leave[start + at * 10 + o, cell] = 1
                enter[window * 64 + o * 8 + place, start + at * 10 + o] = 1
            for t in range(2):
                leave[start + at * 10 + 8 + t, CELLS + t * GROUPS + (i * 4 + j) * 8 + k] = 1
                enter[CELLS + t * GROUPS + window * 8 + place, start + at * 10 + 8 + t] = 1
    return leave, enter


def dot(left, right, left_dim=1, right_dim=0):
    return lax.dot_general(
        left, right, (((left_dim,), (right_dim,)), ((), ())), preferred_element_type=F32
    )


def norm_parts(parts, count):
    average = sum(jnp.sum(p, axis=-1, keepdims=True) for p in parts) * (1.0 / count)
    centred = [p - average for p in parts]
    variance = sum(jnp.sum(p * p, axis=-1, keepdims=True) for p in centred) * (1.0 / count)
    return centred, lax.rsqrt(variance + EPSILON)


def norm_back(hats, grads, inverse, count):
    first = sum(jnp.sum(g, axis=-1, keepdims=True) for g in grads) * (1.0 / count)
    second = sum(jnp.sum(g * h, axis=-1, keepdims=True) for g, h in zip(grads, hats)) * (1.0 / count)
    return [inverse * (g - first - h * second) for g, h in zip(grads, hats)]


def kernel(
    tokens, cotangent, gain_attn, gain_merge, w_qkv_hbm, w_proj_hbm, w_merge_hbm,
    leave_hbm, enter_hbm, back_hbm, home_hbm,
    merged_out, d_tokens_out, d_gain_attn_out, d_qkv_out, d_proj_out, d_gain_merge_out, d_merge_out,
    w_qkv, w_proj, w_merge, leave, enter, back, home, local_sem,
    stacked, halo_send, halo_recv, back_send, back_recv,
    flat, hat, normal, inverse_a, qkv, probs, attended, summed, d_summed, d_attended, d_qkv, heads,
    cot, nm, hat_m, nm_near, cot_near, pair_rows, pair_cot,
    m_sum, m_in1, m_acc1, m_in2, m_acc2, m_in3,
    q_sum, q_near, q_half, q_in1, q_acc1, q_in2, q_acc2, q_in3, q_out,
    g_sum, g_near, g_in1, g_in2, g_in3,
    send_sem, recv_sem,
):
    gx, gy, gz = lax.axis_index("gx"), lax.axis_index("gy"), lax.axis_index("gz")
    x, y_low, z = lax.div(gx, 2), lax.rem(gx, 2), gy
    y_high, core = lax.div(gz, 2), lax.rem(gz, 2)
    y = y_high * 2 + y_low

    def device(x_at, y_at, z_at, core_at):
        return (x_at * 2 + lax.rem(y_at, 2), z_at, lax.div(y_at, 2) * 2 + core_at)

    def along(axis, step):
        if axis == "x":
            return device(lax.rem(x + step, 4), y, z, core)
        if axis == "y":
            return device(x, lax.rem(y + step, 4), z, core)
        return device(x, y, lax.rem(z + step, 8), core)

    other_core = 1 - core
    partner = device(x, y, z, other_core)
    coordinate = {"x": x, "y": y, "z": z}

    def neighbour(kind, sign):
        a, b, c = kind
        return (
            lax.rem(gx + (8 + sign * a), 8),
            lax.rem(gy + (8 + sign * b), 8),
            lax.rem(gz + (4 + sign * c), 4),
        )

    started = []

    def send(source, target, to):
        at = len(started)
        copy = pltpu.make_async_remote_copy(
            src_ref=source, dst_ref=target, send_sem=send_sem.at[at], recv_sem=recv_sem.at[at],
            device_id=to, device_id_type=MESH,
        )
        copy.start()
        started.append(copy)
        return copy

    def arrive(copies):
        for copy in copies:
            copy.wait_recv()

    def rows(at, count):
        return pl.ds(pl.multiple_of(at * count, count), count)

    barrier = pltpu.get_barrier_semaphore()
    partners = [neighbour(kind, sign) for kind in KINDS[1:] for sign in (-1, 1)]
    partners += [partner]
    partners += [along(axis, step) for axis in "xy" for step in (1, 2, 3)]
    partners += [along("z", step) for step in range(1, 8)]
    for there in partners:
        pl.semaphore_signal(barrier, inc=1, device_id=there, device_id_type=MESH)

    loads = {}
    for at, (name, source, target) in enumerate((
        ("leave", leave_hbm, leave), ("enter", enter_hbm, enter), ("w_qkv", w_qkv_hbm, w_qkv),
        ("w_proj", w_proj_hbm, w_proj), ("w_merge", w_merge_hbm, w_merge),
        ("back", back_hbm, back), ("home", home_hbm, home),
    )):
        loads[name] = pltpu.make_async_copy(source, target, local_sem.at[at])
        loads[name].start()

    stacked[0:CELLS, :] = tokens[...]
    stacked[CELLS : CELLS + GROUPS, :] = cotangent[:, 0:WIDTH]
    stacked[CELLS + GROUPS :, :] = cotangent[:, WIDTH:]
    loads["leave"].wait()
    halo_send[...] = dot(leave[...], stacked[...]).astype(BF16)

    pl.semaphore_wait(barrier, len(partners))
    halo = []
    for kind, start, size in list(zip(KINDS, STARTS, SIZES))[1:]:
        block = pl.ds(start, size)
        halo.append(send(halo_send.at[block], halo_recv.at[block], neighbour(kind, -1)))
    halo_recv[0 : SIZES[0], :] = halo_send[0 : SIZES[0], :]
    head_of_lane = lax.div(lax.broadcasted_iota(jnp.int32, (64, WIDTH), 1), 32)
    for h in range(HEADS):
        heads[h * 64 : (h + 1) * 64, :] = jnp.where(head_of_lane == h, 1.0, 0.0).astype(BF16)
    loads["enter"].wait()
    loads["w_qkv"].wait()
    arrive(halo)

    flat[...] = dot(enter[0:CELLS, :], halo_recv[...])
    for t in range(2):
        part = dot(enter[CELLS + t * GROUPS : CELLS + (t + 1) * GROUPS, :], halo_recv[...])
        cot[:, t * WIDTH : (t + 1) * WIDTH] = part.astype(BF16)
    chip = [send(cot, cot_near, partner)]
    (centred,), inverse = norm_parts([flat[...]], WIDTH)
    inverse_a[...] = inverse
    hat[...] = centred * inverse
    normal[...] = (hat[...] * gain_attn[...]).astype(BF16)
    qkv[...] = dot(normal[...], w_qkv[...]).astype(BF16)

    def spread(block):
        return jnp.concatenate([block] * HEADS, axis=0) * heads[...]

    def gather(wide):
        total = wide[0:64]
        for h in range(1, HEADS):
            total = jnp.where(head_of_lane == h, wide[h * 64 : (h + 1) * 64], total)
        return total

    def forward(w, carry):
        here = rows(w, 64)
        query, key, value = (qkv[here, i * WIDTH : (i + 1) * WIDTH] for i in range(3))
        scores = dot(key, spread(query), 1, 1) * FACTOR
        powers = jnp.exp(scores - jnp.max(scores, axis=0, keepdims=True))
        weights = powers * (1.0 / jnp.sum(powers, axis=0, keepdims=True))
        probs[here, :] = weights
        attended[here, :] = gather(dot(weights.astype(BF16), value, 0, 0)).astype(BF16)
        return carry

    lax.fori_loop(0, 8, forward, 0)
    loads["w_proj"].wait()
    summed[...] = (flat[...] + dot(attended[...], w_proj[...])).astype(BF16).astype(F32)

    shaped = summed[...].reshape(8, 8, 8, WIDTH)
    slabs = [shaped[:, o].reshape(GROUPS, WIDTH) for o in range(8)]
    centred, inverse = norm_parts(slabs, 8 * WIDTH)
    for o in range(8):
        lanes = slice(o * WIDTH, (o + 1) * WIDTH)
        hat_m[:, lanes] = centred[o] * inverse
        nm[:, lanes] = (hat_m[:, lanes] * gain_merge[:, lanes]).astype(BF16)
    chip.append(send(nm.at[:, rows(other_core, 1024)], nm_near, partner))
    loads["w_merge"].wait()
    result = dot(nm[...], w_merge[...]).astype(BF16)
    for t in range(2):
        stacked[CELLS + t * GROUPS : CELLS + (t + 1) * GROUPS, :] = result[:, t * WIDTH : (t + 1) * WIDTH]
    hats, grads = [], []
    for o in range(8):
        lanes = slice(o * WIDTH, (o + 1) * WIDTH)
        grad = dot(cot[...], w_merge[lanes, :], 1, 1)
        hats.append(hat_m[:, lanes])
        grads.append(grad * gain_merge[:, lanes])
        g_sum[o : o + 1, :] = jnp.sum(grad * hats[o], axis=0, keepdims=True)
    grads = norm_back(hats, grads, inverse, 8 * WIDTH)
    joined = jnp.stack([g.reshape(8, 8, WIDTH) for g in grads], axis=1).reshape(CELLS, WIDTH)
    d_summed[...] = joined.astype(BF16)

    arrive(chip)
    pair_rows[0:64, :] = nm[:, rows(core, 1024)]
    pair_rows[64:128, :] = nm_near[...]
    pair_cot[0:64, :] = cot[...]
    pair_cot[64:128, :] = cot_near[...]

    def m_block(i, carry):
        here = rows(i, 128)
        m_sum[here, :] = dot(pair_rows[:, here], pair_cot[...], 0, 0)
        return carry

    lax.fori_loop(0, 8, m_block, 0)
    orders = (("x", "y"), ("y", "x"))

    def m_first(half):
        axis = orders[half][0]
        copies = []
        for step in (1, 2, 3):
            chunk = half * 4 + lax.rem(coordinate[axis] + step, 4)
            copies.append(send(m_sum.at[rows(chunk, 128)], m_in1.at[half, step - 1], along(axis, step)))
        return copies

    m_copies = [m_first(0), m_first(1)]

    q_sum[:, 3 * WIDTH :] = dot(attended[...], d_summed[...], 0, 0)
    d_attended[...] = dot(d_summed[...], w_proj[...], 1, 1).astype(BF16)

    def backward(w, carry):
        here = rows(w, 64)
        query, key, value = (qkv[here, i * WIDTH : (i + 1) * WIDTH] for i in range(3))
        weights = probs[here, :]
        wide = spread(d_attended[here, :])
        d_probs = dot(value, wide, 1, 1)
        d_value = dot(weights.astype(BF16), wide)
        inner = jnp.sum(d_probs * weights, axis=0, keepdims=True)
        d_scores = (weights * (d_probs - inner) * FACTOR).astype(BF16)
        d_key = dot(d_scores, spread(query))
        d_query = gather(dot(d_scores, key, 0, 0))
        d_qkv[here, 0:WIDTH] = d_query.astype(BF16)
        d_qkv[here, WIDTH : 2 * WIDTH] = d_key.astype(BF16)
        d_qkv[here, 2 * WIDTH :] = d_value.astype(BF16)
        return carry

    lax.fori_loop(0, 4, backward, 0)

    def m_second(half):
        first, second = orders[half]
        arrive(m_copies[half])
        own = m_sum[rows(half * 4 + coordinate[first], 128), :]
        m_acc1[half] = own + m_in1[half, 0] + m_in1[half, 1] + m_in1[half, 2]
        copies = []
        for step in (1, 2, 3):
            chunk = rows(lax.rem(coordinate[second] + step, 4), 32)
            copies.append(send(m_acc1.at[half, chunk], m_in2.at[half, step - 1], along(second, step)))
        return copies

    m_copies = [m_second(0), m_second(1)]
    lax.fori_loop(4, 8, backward, 0)

    def m_third(half):
        second = orders[half][1]
        arrive(m_copies[half])
        own = m_acc1[half, rows(coordinate[second], 32), :]
        m_acc2[half] = own + m_in2[half, 0] + m_in2[half, 1] + m_in2[half, 2]
        copies = []
        for step in range(1, 8):
            there = lax.rem(z + step, 8)
            chunk = m_acc2.at[half, rows(lax.div(there, 4), 16), rows(lax.rem(there, 4), 128)]
            copies.append(send(chunk, m_in3.at[half, step - 1], along("z", step)))
        return copies

    m_copies = [m_third(0), m_third(1)]

    q_sum[:, 0 : 3 * WIDTH] = dot(normal[...], d_qkv[...], 0, 0)
    q_chip = send(q_sum.at[:, rows(other_core, 512)], q_near, partner)
    d_normal = dot(d_qkv[...], w_qkv[...], 1, 1)
    g_sum[8:16, :] = jnp.zeros((8, WIDTH), F32)
    g_sum[8:9, :] = jnp.sum(d_normal * hat[...], axis=0, keepdims=True)
    g_chip = send(g_sum, g_near, partner)
    (d_flat,) = norm_back([hat[...]], [d_normal * gain_attn[...]], inverse_a[...], WIDTH)
    stacked[0:CELLS, :] = (d_summed[...].astype(F32) + d_flat).astype(BF16)
    loads["back"].wait()
    back_send[...] = dot(back[...], stacked[...]).astype(BF16)
    halo = []
    for kind, start, size in list(zip(KINDS, STARTS, SIZES))[1:]:
        block = pl.ds(start, size)
        halo.append(send(back_send.at[block], back_recv.at[block], neighbour(kind, 1)))
    back_recv[0 : SIZES[0], :] = back_send[0 : SIZES[0], :]

    def m_place(half, x_or_y_first, x_or_y_second):
        return core * 1024 + half * 512 + x_or_y_first * 128 + x_or_y_second * 32

    def m_fourth(half):
        first, second = orders[half]
        arrive(m_copies[half])
        high, lane = lax.div(z, 4), rows(lax.rem(z, 4), 128)
        total = m_acc2[half, rows(high, 16), lane]
        for step in range(7):
            total = total + m_in3[half, step]
        start = m_place(half, coordinate[first], coordinate[second]) + high * 16
        here = (pl.ds(pl.multiple_of(start, 16), 16), lane)
        d_merge_out[here] = (total * MERGE_SCALE).astype(BF16)
        place = d_merge_out.at[here]
        return [send(place, place, along("z", step)) for step in range(1, 8)]

    m_copies = [m_fourth(0), m_fourth(1)]

    q_chip.wait_recv()
    q_half[...] = q_sum[:, rows(core, 512)] + q_near[...]

    def q_first(half):
        axis = orders[half][0]
        copies = []
        for step in (1, 2, 3):
            chunk = half * 4 + lax.rem(coordinate[axis] + step, 4)
            copies.append(send(q_half.at[rows(chunk, 32)], q_in1.at[half, step - 1], along(axis, step)))
        return copies

    q_copies = [q_first(0), q_first(1)]
    g_chip.wait_recv()

    def g_start(total, into, axis, count):
        into[coordinate[axis]] = total
        mine = into.at[coordinate[axis]]
        return [send(mine, mine, along(axis, step)) for step in range(1, count)]

    def g_total(into, count):
        total = into[0]
        for i in range(1, count):
            total = total + into[i]
        return total

    g_copies = g_start(g_sum[...] + g_near[...], g_in1, "x", 4)

    def m_fifth(half):
        first, second = orders[half]
        arrive(m_copies[half])
        start = m_place(half, coordinate[first], coordinate[second])
        place = d_merge_out.at[pl.ds(pl.multiple_of(start, 32), 32)]
        return [send(place, place, along(second, step)) for step in (1, 2, 3)]

    m_copies = [m_fifth(0), m_fifth(1)]

    def q_second(half):
        first, second = orders[half]
        arrive(q_copies[half])
        own = q_half[rows(half * 4 + coordinate[first], 32), :]
        q_acc1[half] = own + q_in1[half, 0] + q_in1[half, 1] + q_in1[half, 2]
        copies = []
        for step in (1, 2, 3):
            lane = rows(lax.rem(coordinate[second] + step, 4), 128)
            copies.append(send(q_acc1.at[half, :, lane], q_in2.at[half, step - 1], along(second, step)))
        return copies

    q_copies = [q_second(0), q_second(1)]
    arrive(g_copies)
    g_copies = g_start(g_total(g_in1, 4), g_in2, "y", 4)

    def m_sixth(half):
        first = orders[half][0]
        arrive(m_copies[half])
        place = d_merge_out.at[rows(core * 8 + half * 4 + coordinate[first], 128)]
        return [send(place, place, along(first, step)) for step in (1, 2, 3)]

    m_copies = [m_sixth(0), m_sixth(1)]

    def q_third(half):
        second = orders[half][1]
        arrive(q_copies[half])
        own = q_acc1[half, :, rows(coordinate[second], 128)]
        q_acc2[half] = own + q_in2[half, 0] + q_in2[half, 1] + q_in2[half, 2]
        q_in3[half, z] = q_acc2[half, rows(lax.rem(z, 2), 16), :]
        copies = []
        for step in range(1, 8):
            chunk = q_acc2.at[half, rows(lax.rem(z + step, 2), 16)]
            copies.append(send(chunk, q_in3.at[half, z], along("z", step)))
        return copies

    q_copies = [q_third(0), q_third(1)]
    arrive(g_copies)
    g_copies = g_start(g_total(g_in2, 4), g_in3, "z", 8)

    loads["home"].wait()
    arrive(halo)
    placed = dot(home[...], back_recv[...]).astype(BF16)
    d_tokens_out[...] = placed[0:CELLS]
    merged_out[:, 0:WIDTH] = placed[CELLS : CELLS + GROUPS]
    merged_out[:, WIDTH:] = placed[CELLS + GROUPS :]

    def q_place(half, first_at):
        return half * 128 + first_at * 32

    def q_fourth(half):
        first, second = orders[half]
        arrive(q_copies[half])
        total = q_in3[half, 0]
        for i in range(1, 8):
            total = total + q_in3[half, i]
        start = q_place(half, coordinate[first]) + lax.rem(z, 2) * 16
        lane = rows(core * 4 + coordinate[second], 128)
        here = (pl.ds(pl.multiple_of(start, 16), 16), lane)
        q_out[here] = (total * TOKEN_SCALE).astype(BF16)
        place = q_out.at[here]
        return [send(place, place, device(x, y, z + 1 - 2 * lax.rem(z, 2), core))]

    q_copies = [q_fourth(0), q_fourth(1)]

    def q_fifth(half):
        first, second = orders[half]
        arrive(q_copies[half])
        start = pl.multiple_of(q_place(half, coordinate[first]), 32)
        place = q_out.at[pl.ds(start, 32), rows(core * 4 + coordinate[second], 128)]
        return [send(place, place, along(second, step)) for step in (1, 2, 3)]

    q_copies = [q_fifth(0), q_fifth(1)]
    arrive(m_copies[0])
    arrive(m_copies[1])
    place = d_merge_out.at[rows(core, 1024)]
    last = [send(place, place, partner)]

    def q_sixth(half):
        first = orders[half][0]
        arrive(q_copies[half])
        start = pl.multiple_of(q_place(half, coordinate[first]), 32)
        place = q_out.at[pl.ds(start, 32), rows(core, 512)]
        return [send(place, place, along(first, step)) for step in (1, 2, 3)]

    q_copies = [q_sixth(0), q_sixth(1)]
    arrive(g_copies)
    total = g_total(g_in3, 8)
    for o in range(8):
        d_gain_merge_out[:, o * WIDTH : (o + 1) * WIDTH] = total[o : o + 1] * MERGE_SCALE
    d_gain_attn_out[...] = total[8:9] * TOKEN_SCALE
    arrive(q_copies[0])
    arrive(q_copies[1])
    place = q_out.at[:, rows(core, 512)]
    last.append(send(place, place, partner))
    arrive(last)
    d_qkv_out[...] = q_out[:, 0 : 3 * WIDTH]
    d_proj_out[...] = q_out[:, 3 * WIDTH :]
    for copy in started:
        copy.wait_send()


def local(leave, enter, back, home, tokens, cotangent, gain_attn, w_qkv, w_proj, gain_merge, w_merge):
    vmem, anywhere = pl.BlockSpec(memory_space=pltpu.VMEM), pl.BlockSpec(memory_space=pl.ANY)
    copies = 200
    outs = pl.pallas_call(
        kernel,
        out_shape=(
            jax.ShapeDtypeStruct((GROUPS, 512), BF16),
            jax.ShapeDtypeStruct((CELLS, WIDTH), BF16),
            jax.ShapeDtypeStruct((1, WIDTH), F32),
            jax.ShapeDtypeStruct((WIDTH, 3 * WIDTH), BF16),
            jax.ShapeDtypeStruct((WIDTH, WIDTH), BF16),
            jax.ShapeDtypeStruct((1, 8 * WIDTH), F32),
            jax.ShapeDtypeStruct((8 * WIDTH, 512), BF16),
        ),
        in_specs=[vmem] * 4 + [anywhere] * 7,
        out_specs=[vmem] * 7,
        scratch_shapes=[
            pltpu.VMEM((WIDTH, 3 * WIDTH), BF16),
            pltpu.VMEM((WIDTH, WIDTH), BF16),
            pltpu.VMEM((8 * WIDTH, 512), BF16),
            pltpu.VMEM((HALO, ROWS), BF16),
            pltpu.VMEM((ROWS, HALO), BF16),
            pltpu.VMEM((HALO, ROWS), BF16),
            pltpu.VMEM((ROWS, HALO), BF16),
            pltpu.SemaphoreType.DMA((7,)),
            pltpu.VMEM((ROWS, WIDTH), BF16),
            pltpu.VMEM((HALO, WIDTH), BF16),
            pltpu.VMEM((HALO, WIDTH), BF16),
            pltpu.VMEM((HALO, WIDTH), BF16),
            pltpu.VMEM((HALO, WIDTH), BF16),
            pltpu.VMEM((CELLS, WIDTH), F32),
            pltpu.VMEM((CELLS, WIDTH), F32),
            pltpu.VMEM((CELLS, WIDTH), BF16),
            pltpu.VMEM((CELLS, 1), F32),
            pltpu.VMEM((CELLS, 3 * WIDTH), BF16),
            pltpu.VMEM((CELLS, 512), F32),
            pltpu.VMEM((CELLS, WIDTH), BF16),
            pltpu.VMEM((CELLS, WIDTH), F32),
            pltpu.VMEM((CELLS, WIDTH), BF16),
            pltpu.VMEM((CELLS, WIDTH), BF16),
            pltpu.VMEM((CELLS, 3 * WIDTH), BF16),
            pltpu.VMEM((CELLS, WIDTH), BF16),
            pltpu.VMEM((GROUPS, 512), BF16),
            pltpu.VMEM((GROUPS, 8 * WIDTH), BF16),
            pltpu.VMEM((GROUPS, 8 * WIDTH), F32),
            pltpu.VMEM((GROUPS, 1024), BF16),
            pltpu.VMEM((GROUPS, 512), BF16),
            pltpu.VMEM((2 * GROUPS, 1024), BF16),
            pltpu.VMEM((2 * GROUPS, 512), BF16),
            pltpu.VMEM((1024, 512), F32),
            pltpu.VMEM((2, 3, 128, 512), F32),
            pltpu.VMEM((2, 128, 512), F32),
            pltpu.VMEM((2, 3, 32, 512), F32),
            pltpu.VMEM((2, 32, 512), F32),
            pltpu.VMEM((2, 7, 16, 128), F32),
            pltpu.VMEM((WIDTH, 1024), F32),
            pltpu.VMEM((WIDTH, 512), F32),
            pltpu.VMEM((WIDTH, 512), F32),
            pltpu.VMEM((2, 3, 32, 512), F32),
            pltpu.VMEM((2, 32, 512), F32),
            pltpu.VMEM((2, 3, 32, 128), F32),
            pltpu.VMEM((2, 32, 128), F32),
            pltpu.VMEM((2, 8, 16, 128), F32),
            pltpu.VMEM((WIDTH, 1024), BF16),
            pltpu.VMEM((16, WIDTH), F32),
            pltpu.VMEM((16, WIDTH), F32),
            pltpu.VMEM((4, 16, WIDTH), F32),
            pltpu.VMEM((4, 16, WIDTH), F32),
            pltpu.VMEM((8, 16, WIDTH), F32),
            pltpu.SemaphoreType.DMA((copies,)),
            pltpu.SemaphoreType.DMA((copies,)),
        ],
        compiler_params=pltpu.CompilerParams(
            collective_id=0, has_side_effects=True, vmem_limit_bytes=48 * 1024 * 1024
        ),
        cost_estimate=pl.CostEstimate(flops=4 * 10**9, bytes_accessed=12 * 10**6, transcendentals=262144),
        name="window_step",
    )(
        tokens.reshape(CELLS, WIDTH), cotangent.reshape(GROUPS, 512),
        gain_attn.reshape(1, WIDTH), gain_merge.reshape(1, 8 * WIDTH),
        w_qkv, w_proj, w_merge, leave, enter, back, home,
    )
    merged, d_tokens, d_gain_attn, d_qkv, d_proj, d_gain_merge, d_merge = outs
    return (
        merged.reshape(cotangent.shape), d_tokens.reshape(tokens.shape), d_gain_attn.reshape(WIDTH),
        d_qkv, d_proj, d_gain_merge.reshape(8 * WIDTH), d_merge,
    )


def solution(mesh):
    leave, enter = orderings()
    constants = [jnp.asarray(m, BF16) for m in (leave, enter, enter.T, leave.T)]
    box, whole = P("gx", "gy", "gz", None), P()
    return jax.shard_map(
        functools.partial(local, *constants),
        mesh=mesh,
        in_specs=(box, box, whole, whole, whole, whole, whole),
        out_specs=(box, box, whole, whole, whole, whole, whole),
        check_vma=False,
    )
```

time: 406 us -> 102 us (0.25)
  waiting for transfers between devices: 206 us -> 0 us
  Pallas kernels: 0 us -> 84.2 us
  blocking collectives: 77.4 us -> 0 us
  matrix products: 35.4 us -> 0 us
  starting transfers between devices: 24.1 us -> 0 us
  other arithmetic: 17.5 us -> 0 us
  between operations: 14.6 us -> 0.66 us
  local copies, waits for them, and re-layouts: 29 us -> 16.7 us
    psum x1 -> x0, waiting for transfers between devices: 177 us -> none  [local(): lax.psum((grad_ga, grad_wq, grad_wp, grad_gm, grad_wm), ('gx', 'gy', 'gz'))]
    pallas_call x0 -> x1, Pallas kernels: none -> 84.2 us  [local(): pl.pallas_call(kernel, out_shape=(jax.ShapeDtypeStruct((GROUPS, 512), BF1...]
    psum x1 -> x0, blocking collectives: 77.4 us -> none  [local(): lax.psum((grad_ga, grad_wq, grad_wp, grad_gm, grad_wm), ('gx', 'gy', 'gz'))]
    dot_general x14 -> x0, matrix products: 31.9 us -> none  [the longest x5 17.4 us: batched(): jnp.einsum(form, left_side, right_side, preferred_element_type=jnp.float32)]
    ppermute x12 -> x0, waiting for transfers between devices: 29.6 us -> none  [shifted(): return lax.ppermute(block, axis, route)]
    ppermute x12 -> x0, starting transfers between devices: 24.1 us -> none  [shifted(): return lax.ppermute(block, axis, route)]
    unnamed x50 -> x27, local copies, waits for them, and re-layouts: 1.69 us -> 16.7 us
    convert_element_type x13 -> x0, local copies, waits for them, and re-layouts: 14.3 us -> none  [the longest x2 5.61 us: attend_backward(): grad_project = jnp.stack([grad_queries, grad_keys, grad_values], axis=2)....]
  transfers between devices with their start and end apart: 13 -> 0, of which waited for: 11 -> 0; matrix products, arithmetic and copies ran while one was open for 3% -> 0% of each run, Pallas kernels for 0% -> 0%
where the time goes in v1:
time: 102 us
  Pallas kernels  84.2 us (83%)
  local copies, waits for them, and re-layouts  16.7 us (16%)
    pallas_call x1, Pallas kernels, local(): pl.pallas_call(kernel, out_shape=(jax.ShapeDtypeStruct((GROUPS, 512), BF1...  84.2 us
    unnamed x27, local copies, waits for them, and re-layouts  16.7 us

profile of v1, /device:TPU:1, one launch (start us, length us, event | category | flops | bytes accessed | tf_op | source)
XLA Modules:
  0.0 101.6 jit_solution(6219311572188355328)
XLA Ops:
  0.6 0.0 copy-start
  0.6 1.0 copy-done
  1.6 0.0 copy-start.1
  1.6 0.9 copy-done.1
  2.6 0.0 copy-start.2
  2.6 0.9 copy-done.2
  3.5 0.0 copy-start.3
  3.5 0.8 copy-done.3
  4.3 0.0 copy-start.4
  4.3 0.7 copy-done.4
  5.0 0.0 copy-start.5
  5.0 0.7 copy-done.5
  5.7 0.0 copy-start.6
  5.7 1.2 %copy-done.6 = bf16[640,704]{1,0:T(8,128)(2,1)S(1)} copy-done((bf16[640,704]{1,0:T(8,128)(2,1)S(1)}, bf16[640,704]{1,0:T(8,128)(2,1)}, u32[]{:S(2)}) %copy-start.6) | copy-done | bytes 901144
  6.9 0.0 copy-start.7
  6.9 1.2 %copy-done.7 = bf16[640,704]{1,0:T(8,128)(2,1)S(1)} copy-done((bf16[640,704]{1,0:T(8,128)(2,1)S(1)}, bf16[640,704]{1,0:T(8,128)(2,1)}, u32[]{:S(2)}) %copy-start.7) | copy-done | bytes 901144
  8.1 0.0 copy-start.8
  8.1 1.2 %copy-done.8 = bf16[704,640]{1,0:T(8,128)(2,1)S(1)} copy-done((bf16[704,640]{1,0:T(8,128)(2,1)S(1)}, bf16[704,640]{1,0:T(8,128)(2,1)}, u32[]{:S(2)}) %copy-start.8) | copy-done | bytes 901144
  9.3 0.0 copy-start.9
  9.3 1.2 %copy-done.9 = bf16[704,640]{1,0:T(8,128)(2,1)S(1)} copy-done((bf16[704,640]{1,0:T(8,128)(2,1)S(1)}, bf16[704,640]{1,0:T(8,128)(2,1)}, u32[]{:S(2)}) %copy-start.9) | copy-done | bytes 901144
  10.5 84.2 %window_step.1 = (bf16[64,512]{1,0:T(8,128)(2,1)S(1)}, bf16[512,256]{1,0:T(8,128)(2,1)S(1)}, f32[1,256]{1,0:T(1,128)S(1)}, bf16[256,768]{1,0:T(8,128)(2,1)S(1)},...) custom-call(bf16[512,256]{1,0:T(8,128)(2,1)S(1)} %bitcast.12, ...), custom_call_target="tpu_custom_call" | custom-call | flops 4000000000 | bytes 12000000 | tf_op jit(solution)/shard_map/window_step/pallas_call | solution.py:476
  94.7 0.6 copy.25
  95.3 0.7 copy.26
  96.0 0.6 copy.27
  96.6 0.7 copy.28
  97.3 0.7 copy.29
  98.0 0.6 copy.30
  98.6 3.0 %copy.31 = bf16[2048,512]{1,0:T(8,128)(2,1)} copy(bf16[2048,512]{1,0:T(8,128)(2,1)} %get-tuple-element.34) | data formatting | bytes 4194304
Async XLA Ops:
  0.6 1.0 copy-start
  1.6 0.9 copy-start.1
  2.6 0.9 copy-start.2
  3.5 0.8 copy-start.3
  4.3 0.7 copy-start.4
  5.0 0.7 copy-start.5
  5.7 1.2 %copy-start.6 = (bf16[640,704]{1,0:T(8,128)(2,1)S(1)}, bf16[640,704]{1,0:T(8,128)(2,1)}, u32[]{:S(2)}) copy-start(bf16[640,704]{1,0:T(8,128)(2,1)} %constant.11.clone.home_hbm) | copy-start | bytes 2703364
  6.9 1.2 %copy-start.7 = (bf16[640,704]{1,0:T(8,128)(2,1)S(1)}, bf16[640,704]{1,0:T(8,128)(2,1)}, u32[]{:S(2)}) copy-start(bf16[640,704]{1,0:T(8,128)(2,1)} %constant.9.clone.enter_hbm) | copy-start | bytes 2703364
  8.1 1.2 %copy-start.8 = (bf16[704,640]{1,0:T(8,128)(2,1)S(1)}, bf16[704,640]{1,0:T(8,128)(2,1)}, u32[]{:S(2)}) copy-start(bf16[704,640]{1,0:T(8,128)(2,1)} %constant.10.clone.back_hbm) | copy-start | bytes 2703364
  9.3 1.2 %copy-start.9 = (bf16[704,640]{1,0:T(8,128)(2,1)S(1)}, bf16[704,640]{1,0:T(8,128)(2,1)}, u32[]{:S(2)}) copy-start(bf16[704,640]{1,0:T(8,128)(2,1)} %constant.8.clone.leave_hbm) | copy-start | bytes 2703364

commit v2 on v1

--- a/solution.py
+++ b/solution.py
@@ -75,14 +75,13 @@
 
 
 def kernel(
-    tokens, cotangent, gain_attn, gain_merge, w_qkv_hbm, w_proj_hbm, w_merge_hbm,
+    tokens_hbm, cotangent_hbm, gain_attn_hbm, gain_merge_hbm, w_qkv_hbm, w_proj_hbm, w_merge_hbm,
     leave_hbm, enter_hbm, back_hbm, home_hbm,
     merged_out, d_tokens_out, d_gain_attn_out, d_qkv_out, d_proj_out, d_gain_merge_out, d_merge_out,
-    w_qkv, w_proj, w_merge, leave, enter, back, home, local_sem,
+    cotangent, gain_attn, gain_merge, w_qkv, w_proj, w_merge, leave, enter, back, home, local_sem,
     stacked, halo_send, halo_recv, back_send, back_recv,
     flat, hat, normal, inverse_a, qkv, probs, attended, summed, d_summed, d_attended, d_qkv, heads,
-    cot, nm, hat_m, nm_near, cot_near, pair_rows, pair_cot,
-    m_sum, m_in1, m_acc1, m_in2, m_acc2, m_in3,
+    cot, nm, hat_m, m_nm, m_cot, m_acc1, m_in2, m_acc2, m_in3,
     q_sum, q_near, q_half, q_in1, q_acc1, q_in2, q_acc2, q_in3, q_out,
     g_sum, g_near, g_in1, g_in2, g_in3,
     send_sem, recv_sem,
@@ -95,14 +94,15 @@
     def device(x_at, y_at, z_at, core_at):
         return (x_at * 2 + lax.rem(y_at, 2), z_at, lax.div(y_at, 2) * 2 + core_at)
 
-    def along(axis, step):
+    other_core = 1 - core
+
+    def along(axis, step, core_at=core):
         if axis == "x":
-            return device(lax.rem(x + step, 4), y, z, core)
+            return device(lax.rem(x + step, 4), y, z, core_at)
         if axis == "y":
-            return device(x, lax.rem(y + step, 4), z, core)
-        return device(x, y, lax.rem(z + step, 8), core)
-
-    other_core = 1 - core
+            return device(x, lax.rem(y + step, 4), z, core_at)
+        return device(x, y, lax.rem(z + step, 8), core_at)
+
     partner = device(x, y, z, other_core)
     coordinate = {"x": x, "y": y, "z": z}
 
@@ -137,22 +137,27 @@
     partners = [neighbour(kind, sign) for kind in KINDS[1:] for sign in (-1, 1)]
     partners += [partner]
     partners += [along(axis, step) for axis in "xy" for step in (1, 2, 3)]
+    partners += [along(axis, step, other_core) for axis in "xy" for step in (1, 2, 3)]
     partners += [along("z", step) for step in range(1, 8)]
     for there in partners:
         pl.semaphore_signal(barrier, inc=1, device_id=there, device_id_type=MESH)
 
     loads = {}
     for at, (name, source, target) in enumerate((
-        ("leave", leave_hbm, leave), ("enter", enter_hbm, enter), ("w_qkv", w_qkv_hbm, w_qkv),
+        ("leave", leave_hbm, leave), ("tokens", tokens_hbm, stacked.at[pl.ds(0, CELLS)]),
+        ("cotangent", cotangent_hbm, cotangent), ("gain_attn", gain_attn_hbm, gain_attn),
+        ("gain_merge", gain_merge_hbm, gain_merge),
+        ("enter", enter_hbm, enter), ("w_qkv", w_qkv_hbm, w_qkv),
         ("w_proj", w_proj_hbm, w_proj), ("w_merge", w_merge_hbm, w_merge),
         ("back", back_hbm, back), ("home", home_hbm, home),
     )):
         loads[name] = pltpu.make_async_copy(source, target, local_sem.at[at])
         loads[name].start()
 
-    stacked[0:CELLS, :] = tokens[...]
+    loads["cotangent"].wait()
     stacked[CELLS : CELLS + GROUPS, :] = cotangent[:, 0:WIDTH]
     stacked[CELLS + GROUPS :, :] = cotangent[:, WIDTH:]
+    loads["tokens"].wait()
     loads["leave"].wait()
     halo_send[...] = dot(leave[...], stacked[...]).astype(BF16)
 
@@ -167,13 +172,23 @@
         heads[h * 64 : (h + 1) * 64, :] = jnp.where(head_of_lane == h, 1.0, 0.0).astype(BF16)
     loads["enter"].wait()
     loads["w_qkv"].wait()
+    loads["gain_attn"].wait()
+    loads["gain_merge"].wait()
     arrive(halo)
 
     flat[...] = dot(enter[0:CELLS, :], halo_recv[...])
     for t in range(2):
         part = dot(enter[CELLS + t * GROUPS : CELLS + (t + 1) * GROUPS, :], halo_recv[...])
         cot[:, t * WIDTH : (t + 1) * WIDTH] = part.astype(BF16)
-    chip = [send(cot, cot_near, partner)]
+    members = [(step, flip) for step in range(4) for flip in (0, 1)]
+    orders = (("x", "y"), ("y", "x"))
+    m_cot[0, 0:GROUPS, :] = cot[...]
+    m_cot[1, 0:GROUPS, :] = cot[...]
+    m_cots = []
+    for at, (step, flip) in list(enumerate(members))[1:]:
+        for half in (0, 1):
+            there = along(orders[half][0], step, (core, other_core)[flip])
+            m_cots.append(send(cot, m_cot.at[half, pl.ds(at * GROUPS, GROUPS)], there))
     (centred,), inverse = norm_parts([flat[...]], WIDTH)
     inverse_a[...] = inverse
     hat[...] = centred * inverse
@@ -210,7 +225,16 @@
         lanes = slice(o * WIDTH, (o + 1) * WIDTH)
         hat_m[:, lanes] = centred[o] * inverse
         nm[:, lanes] = (hat_m[:, lanes] * gain_merge[:, lanes]).astype(BF16)
-    chip.append(send(nm.at[:, rows(other_core, 1024)], nm_near, partner))
+    m_rows = []
+    for at, (step, flip) in enumerate(members):
+        for half in (0, 1):
+            axis, core_at = orders[half][0], (core, other_core)[flip]
+            block = rows(half * 8 + core_at * 4 + lax.rem(coordinate[axis] + step, 4), 128)
+            if at == 0:
+                m_nm[half, 0:GROUPS, :] = nm[:, block]
+            else:
+                target = m_nm.at[half, pl.ds(at * GROUPS, GROUPS)]
+                m_rows.append(send(nm.at[:, block], target, along(axis, step, core_at)))
     loads["w_merge"].wait()
     result = dot(nm[...], w_merge[...]).astype(BF16)
     for t in range(2):
@@ -225,30 +249,6 @@
     grads = norm_back(hats, grads, inverse, 8 * WIDTH)
     joined = jnp.stack([g.reshape(8, 8, WIDTH) for g in grads], axis=1).reshape(CELLS, WIDTH)
     d_summed[...] = joined.astype(BF16)
-
-    arrive(chip)
-    pair_rows[0:64, :] = nm[:, rows(core, 1024)]
-    pair_rows[64:128, :] = nm_near[...]
-    pair_cot[0:64, :] = cot[...]
-    pair_cot[64:128, :] = cot_near[...]
-
-    def m_block(i, carry):
-        here = rows(i, 128)
-        m_sum[here, :] = dot(pair_rows[:, here], pair_cot[...], 0, 0)
-        return carry
-
-    lax.fori_loop(0, 8, m_block, 0)
-    orders = (("x", "y"), ("y", "x"))
-
-    def m_first(half):
-        axis = orders[half][0]
-        copies = []
-        for step in (1, 2, 3):
-            chunk = half * 4 + lax.rem(coordinate[axis] + step, 4)
-            copies.append(send(m_sum.at[rows(chunk, 128)], m_in1.at[half, step - 1], along(axis, step)))
-        return copies
-
-    m_copies = [m_first(0), m_first(1)]
 
     q_sum[:, 3 * WIDTH :] = dot(attended[...], d_summed[...], 0, 0)
     d_attended[...] = dot(d_summed[...], w_proj[...], 1, 1).astype(BF16)
@@ -269,13 +269,12 @@
         d_qkv[here, 2 * WIDTH :] = d_value.astype(BF16)
         return carry
 
-    lax.fori_loop(0, 4, backward, 0)
+    arrive(m_cots)
+    arrive(m_rows)
 
     def m_second(half):
-        first, second = orders[half]
-        arrive(m_copies[half])
-        own = m_sum[rows(half * 4 + coordinate[first], 128), :]
-        m_acc1[half] = own + m_in1[half, 0] + m_in1[half, 1] + m_in1[half, 2]
+        second = orders[half][1]
+        m_acc1[half] = dot(m_nm[half], m_cot[half], 0, 0)
         copies = []
         for step in (1, 2, 3):
             chunk = rows(lax.rem(coordinate[second] + step, 4), 32)
@@ -283,7 +282,7 @@
         return copies
 
     m_copies = [m_second(0), m_second(1)]
-    lax.fori_loop(4, 8, backward, 0)
+    lax.fori_loop(0, 8, backward, 0)
 
     def m_third(half):
         second = orders[half][1]
@@ -316,7 +315,7 @@
     back_recv[0 : SIZES[0], :] = back_send[0 : SIZES[0], :]
 
     def m_place(half, x_or_y_first, x_or_y_second):
-        return core * 1024 + half * 512 + x_or_y_first * 128 + x_or_y_second * 32
+        return half * 1024 + core * 512 + x_or_y_first * 128 + x_or_y_second * 32
 
     def m_fourth(half):
         first, second = orders[half]
@@ -387,9 +386,11 @@
     def m_sixth(half):
         first = orders[half][0]
         arrive(m_copies[half])
-        place = d_merge_out.at[rows(core * 8 + half * 4 + coordinate[first], 128)]
-        return [send(place, place, along(first, step)) for step in (1, 2, 3)]
-
+        place = d_merge_out.at[rows(half * 8 + core * 4 + coordinate[first], 128)]
+        last.append(send(place, place, partner))
+        return [send(place, place, along(first, step)) for step in (1, 3, 2)]
+
+    last = []
     m_copies = [m_sixth(0), m_sixth(1)]
 
     def q_third(half):
@@ -397,12 +398,8 @@
         arrive(q_copies[half])
         own = q_acc1[half, :, rows(coordinate[second], 128)]
         q_acc2[half] = own + q_in2[half, 0] + q_in2[half, 1] + q_in2[half, 2]
-        q_in3[half, z] = q_acc2[half, rows(lax.rem(z, 2), 16), :]
-        copies = []
-        for step in range(1, 8):
-            chunk = q_acc2.at[half, rows(lax.rem(z + step, 2), 16)]
-            copies.append(send(chunk, q_in3.at[half, z], along("z", step)))
-        return copies
+        q_in3[half, z] = q_acc2[half]
+        return [send(q_acc2.at[half], q_in3.at[half, z], along("z", step)) for step in range(1, 8)]
 
     q_copies = [q_third(0), q_third(1)]
     arrive(g_copies)
@@ -418,33 +415,25 @@
     def q_place(half, first_at):
         return half * 128 + first_at * 32
 
-    def q_fourth(half):
+    def q_fifth(half):
         first, second = orders[half]
         arrive(q_copies[half])
         total = q_in3[half, 0]
         for i in range(1, 8):
             total = total + q_in3[half, i]
-        start = q_place(half, coordinate[first]) + lax.rem(z, 2) * 16
-        lane = rows(core * 4 + coordinate[second], 128)
-        here = (pl.ds(pl.multiple_of(start, 16), 16), lane)
+        start = pl.multiple_of(q_place(half, coordinate[first]), 32)
+        here = (pl.ds(start, 32), rows(core * 4 + coordinate[second], 128))
         q_out[here] = (total * TOKEN_SCALE).astype(BF16)
         place = q_out.at[here]
-        return [send(place, place, device(x, y, z + 1 - 2 * lax.rem(z, 2), core))]
-
-    q_copies = [q_fourth(0), q_fourth(1)]
-
-    def q_fifth(half):
-        first, second = orders[half]
-        arrive(q_copies[half])
-        start = pl.multiple_of(q_place(half, coordinate[first]), 32)
-        place = q_out.at[pl.ds(start, 32), rows(core * 4 + coordinate[second], 128)]
         return [send(place, place, along(second, step)) for step in (1, 2, 3)]
 
     q_copies = [q_fifth(0), q_fifth(1)]
-    arrive(m_copies[0])
-    arrive(m_copies[1])
-    place = d_merge_out.at[rows(core, 1024)]
-    last = [send(place, place, partner)]
+    for at, step in enumerate((1, 3, 2)):
+        for half in (0, 1):
+            arrive([m_copies[half][at]])
+            came = lax.rem(coordinate[orders[half][0]] + 4 - step, 4)
+            place = d_merge_out.at[rows(half * 8 + core * 4 + came, 128)]
+            last.append(send(place, place, partner))
 
     def q_sixth(half):
         first = orders[half][0]
@@ -470,10 +459,29 @@
         copy.wait_send()
 
 
+def hand_out(*refs):
+    given, outs, held, sems = refs[:7], refs[7:14], refs[14:21], refs[21]
+    parts = [(i, None) for i in range(6)] + [(6, pl.ds(at * 512, 512)) for at in range(4)]
+    both = []
+    for at, (i, part) in enumerate(parts):
+        source, stage, target = (r[i] if part is None else r[i].at[part] for r in (given, held, outs))
+        both.append((
+            pltpu.make_async_copy(source, stage, sems.at[0, at]),
+            pltpu.make_async_copy(stage, target, sems.at[1, at]),
+        ))
+    for copy_in, _ in both[::-1]:
+        copy_in.start()
+    for copy_in, copy_out in both[::-1]:
+        copy_in.wait()
+        copy_out.start()
+    for _, copy_out in both:
+        copy_out.wait()
+
+
 def local(leave, enter, back, home, tokens, cotangent, gain_attn, w_qkv, w_proj, gain_merge, w_merge):
-    vmem, anywhere = pl.BlockSpec(memory_space=pltpu.VMEM), pl.BlockSpec(memory_space=pl.ANY)
+    vmem, hbm = pl.BlockSpec(memory_space=pltpu.VMEM), pl.BlockSpec(memory_space=pltpu.HBM)
     copies = 200
-    outs = pl.pallas_call(
+    held = pl.pallas_call(
         kernel,
         out_shape=(
             jax.ShapeDtypeStruct((GROUPS, 512), BF16),
@@ -484,9 +492,12 @@
             jax.ShapeDtypeStruct((1, 8 * WIDTH), F32),
             jax.ShapeDtypeStruct((8 * WIDTH, 512), BF16),
         ),
-        in_specs=[vmem] * 4 + [anywhere] * 7,
+        in_specs=[hbm] * 11,
         out_specs=[vmem] * 7,
         scratch_shapes=[
+            pltpu.VMEM((GROUPS, 512), BF16),
+            pltpu.VMEM((1, WIDTH), F32),
+            pltpu.VMEM((1, 8 * WIDTH), F32),
             pltpu.VMEM((WIDTH, 3 * WIDTH), BF16),
             pltpu.VMEM((WIDTH, WIDTH), BF16),
             pltpu.VMEM((8 * WIDTH, 512), BF16),
@@ -494,7 +505,7 @@
             pltpu.VMEM((ROWS, HALO), BF16),
             pltpu.VMEM((HALO, ROWS), BF16),
             pltpu.VMEM((ROWS, HALO), BF16),
-            pltpu.SemaphoreType.DMA((7,)),
+            pltpu.SemaphoreType.DMA((11,)),
             pltpu.VMEM((ROWS, WIDTH), BF16),
             pltpu.VMEM((HALO, WIDTH), BF16),
             pltpu.VMEM((HALO, WIDTH), BF16),
@@ -515,12 +526,8 @@
             pltpu.VMEM((GROUPS, 512), BF16),
             pltpu.VMEM((GROUPS, 8 * WIDTH), BF16),
             pltpu.VMEM((GROUPS, 8 * WIDTH), F32),
-            pltpu.VMEM((GROUPS, 1024), BF16),
-            pltpu.VMEM((GROUPS, 512), BF16),
-            pltpu.VMEM((2 * GROUPS, 1024), BF16),
-            pltpu.VMEM((2 * GROUPS, 512), BF16),
-            pltpu.VMEM((1024, 512), F32),
-            pltpu.VMEM((2, 3, 128, 512), F32),
+            pltpu.VMEM((2, 8 * GROUPS, 128), BF16),
+            pltpu.VMEM((2, 8 * GROUPS, 512), BF16),
             pltpu.VMEM((2, 128, 512), F32),
             pltpu.VMEM((2, 3, 32, 512), F32),
             pltpu.VMEM((2, 32, 512), F32),
@@ -532,7 +539,7 @@
             pltpu.VMEM((2, 32, 512), F32),
             pltpu.VMEM((2, 3, 32, 128), F32),
             pltpu.VMEM((2, 32, 128), F32),
-            pltpu.VMEM((2, 8, 16, 128), F32),
+            pltpu.VMEM((2, 8, 32, 128), F32),
             pltpu.VMEM((WIDTH, 1024), BF16),
             pltpu.VMEM((16, WIDTH), F32),
             pltpu.VMEM((16, WIDTH), F32),
@@ -543,7 +550,7 @@
             pltpu.SemaphoreType.DMA((copies,)),
         ],
         compiler_params=pltpu.CompilerParams(
-            collective_id=0, has_side_effects=True, vmem_limit_bytes=48 * 1024 * 1024
+            collective_id=0, has_side_effects=True, vmem_limit_bytes=60 * 1024 * 1024
         ),
         cost_estimate=pl.CostEstimate(flops=4 * 10**9, bytes_accessed=12 * 10**6, transcendentals=262144),
         name="window_step",
@@ -552,6 +559,15 @@
         gain_attn.reshape(1, WIDTH), gain_merge.reshape(1, 8 * WIDTH),
         w_qkv, w_proj, w_merge, leave, enter, back, home,
     )
+    outs = pl.pallas_call(
+        hand_out,
+        out_shape=[jax.ShapeDtypeStruct(h.shape, h.dtype) for h in held],
+        in_specs=[pl.BlockSpec(memory_space=pl.ANY)] * 7,
+        out_specs=[hbm] * 7,
+        scratch_shapes=[pltpu.VMEM(h.shape, h.dtype) for h in held] + [pltpu.SemaphoreType.DMA((2, 10))],
+        compiler_params=pltpu.CompilerParams(vmem_limit_bytes=60 * 1024 * 1024),
+        name="hand_out",
+    )(*held)
     merged, d_tokens, d_gain_attn, d_qkv, d_proj, d_gain_merge, d_merge = outs
     return (
         merged.reshape(cotangent.shape), d_tokens.reshape(tokens.shape), d_gain_attn.reshape(WIDTH),

time: 102 us -> 75.9 us (0.74)
  local copies, waits for them, and re-layouts: 16.7 us -> 0 us
  Pallas kernels: 84.2 us -> 75.2 us
    unnamed x27 -> x0, local copies, waits for them, and re-layouts: 16.7 us -> none
    pallas_call x1, Pallas kernels: 84.2 us -> 72.4 us  [local(): pl.pallas_call(kernel, out_shape=(jax.ShapeDtypeStruct((GROUPS, 512), BF1...]
    pallas_call x0 -> x1, Pallas kernels: none -> 2.82 us  [local(): pl.pallas_call(hand_out, out_shape=[jax.ShapeDtypeStruct(h.shape, h.dtype...]
where the time goes in v2:
time: 75.9 us; the launch traced here: 75.8 us
  Pallas kernels  75.2 us (99%)
    pallas_call x1, Pallas kernels, local(): pl.pallas_call(kernel, out_shape=(jax.ShapeDtypeStruct((GROUPS, 512), BF1...  72.4 us
    pallas_call x1, Pallas kernels, local(): pl.pallas_call(hand_out, out_shape=[jax.ShapeDtypeStruct(h.shape, h.dtype...  2.82 us

profile of v2, /device:TPU:1, one launch (start us, length us, event | category | flops | bytes accessed | tf_op | source)
XLA Modules:
  0.0 75.8 jit_solution(12858252081721990142)
XLA Ops:
  0.6 72.4 %window_step.1 = (bf16[64,512]{1,0:T(8,128)(2,1)}, bf16[512,256]{1,0:T(8,128)(2,1)}, f32[1,256]{1,0:T(1,128)}, bf16[256,768]{1,0:T(8,128)(2,1)}, bf16[256,256]{1...) custom-call(bf16[512,256]{1,0:T(8,128)(2,1)} %bitcast.8, bf16[64,512]{1,0:T(8,128)(2,1)} %bitcast.10, ...), custom_call_target="tpu_custom_call" | custom-call | flops 4000000000 | bytes 12000000 | tf_op jit(solution)/shard_map/window_step/pallas_call | solution.py:484
  73.0 2.8 %hand_out.1 = (bf16[64,512]{1,0:T(8,128)(2,1)}, bf16[512,256]{1,0:T(8,128)(2,1)}, f32[1,256]{1,0:T(1,128)}, bf16[256,768]{1,0:T(8,128)(2,1)}, bf16[256,256]{1,0:...) custom-call(bf16[64,512]{1,0:T(8,128)(2,1)} %get-tuple-element.21.refs_0_, ...), custom_call_target="tpu_custom_call" | custom-call | tf_op jit(solution)/shard_map/hand_out/pallas_call | solution.py:562

commit v3 on v2

--- a/solution.py
+++ b/solution.py
@@ -16,6 +16,7 @@
 ROWS = CELLS + 2 * GROUPS
 FACTOR = 32 ** -0.5
 EPSILON = 1e-05
+TOGETHER = 2
 TOKENS = 131072
 TOKEN_SCALE = float(TOKENS) ** (-0.5)
 MERGE_SCALE = float(TOKENS // 8) ** (-0.5)
@@ -40,19 +41,30 @@
 
 
 def orderings():
-    leave, enter = np.zeros((HALO, ROWS), np.float32), np.zeros((ROWS, HALO), np.float32)
+    leave, enter = np.full(ROWS, -1, np.int32), np.full(HALO, -1, np.int32)
+    back, home = np.full(ROWS, -1, np.int32), np.full(HALO, -1, np.int32)
+
+    def pair(natural, place, windowed):
+        leave[natural], enter[place] = place, windowed
+        back[windowed], home[place] = place, natural
+
     for kind, start in zip(KINDS, STARTS):
         for at, (i, j, k) in enumerate(kind_groups(kind)):
             si, sj, sk = (i - 1) % 2, (j - 1) % 4, (k - 1) % 8
             window, place = (sj // 2) * 4 + sk // 2, si * 4 + (sj % 2) * 2 + sk % 2
             for o in range(8):
                 cell = ((2 * i + o // 4) * 8 + 2 * j + o // 2 % 2) * 16 + 2 * k + o % 2
-                leave[start + at * 10 + o, cell] = 1
-                enter[window * 64 + o * 8 + place, start + at * 10 + o] = 1
+                pair(cell, start + at * 10 + o, window * 64 + o * 8 + place)
             for t in range(2):
-                leave[start + at * 10 + 8 + t, CELLS + t * GROUPS + (i * 4 + j) * 8 + k] = 1
-                enter[CELLS + t * GROUPS + window * 8 + place, start + at * 10 + 8 + t] = 1
-    return leave, enter
+                base = CELLS + t * GROUPS
+                pair(base + (i * 4 + j) * 8 + k, start + at * 10 + 8 + t, base + window * 8 + place)
+    return leave, enter, back, home
+
+
+def one_hot(rows_of_columns, height):
+    width = rows_of_columns.shape[1]
+    ids = lax.broadcasted_iota(jnp.int32, (height, width), 0)
+    return jnp.where(ids == rows_of_columns, 1.0, 0.0).astype(BF16)
 
 
 def dot(left, right, left_dim=1, right_dim=0):
@@ -76,14 +88,15 @@
 
 def kernel(
     tokens_hbm, cotangent_hbm, gain_attn_hbm, gain_merge_hbm, w_qkv_hbm, w_proj_hbm, w_merge_hbm,
-    leave_hbm, enter_hbm, back_hbm, home_hbm,
+    leave_map, enter_map, back_map, home_map,
     merged_out, d_tokens_out, d_gain_attn_out, d_qkv_out, d_proj_out, d_gain_merge_out, d_merge_out,
     cotangent, gain_attn, gain_merge, w_qkv, w_proj, w_merge, leave, enter, back, home, local_sem,
     stacked, halo_send, halo_recv, back_send, back_recv,
     flat, hat, normal, inverse_a, qkv, probs, attended, summed, d_summed, d_attended, d_qkv, heads,
     cot, nm, hat_m, m_nm, m_cot, m_acc1, m_in2, m_acc2, m_in3,
-    q_sum, q_near, q_half, q_in1, q_acc1, q_in2, q_acc2, q_in3, q_out,
+    q_sum, q_near, q_half, q_in1, q_acc1, q_in2, q_in3, q_out,
     g_sum, g_near, g_in1, g_in2, g_in3,
+    merged, d_tokens, d_gain_attn, d_gain_merge, d_merge, out_sem,
     send_sem, recv_sem,
 ):
     gx, gy, gz = lax.axis_index("gx"), lax.axis_index("gy"), lax.axis_index("gz")
@@ -144,21 +157,20 @@
 
     loads = {}
     for at, (name, source, target) in enumerate((
-        ("leave", leave_hbm, leave), ("tokens", tokens_hbm, stacked.at[pl.ds(0, CELLS)]),
+        ("tokens", tokens_hbm, stacked.at[pl.ds(0, CELLS)]),
         ("cotangent", cotangent_hbm, cotangent), ("gain_attn", gain_attn_hbm, gain_attn),
         ("gain_merge", gain_merge_hbm, gain_merge),
-        ("enter", enter_hbm, enter), ("w_qkv", w_qkv_hbm, w_qkv),
+        ("w_qkv", w_qkv_hbm, w_qkv),
         ("w_proj", w_proj_hbm, w_proj), ("w_merge", w_merge_hbm, w_merge),
-        ("back", back_hbm, back), ("home", home_hbm, home),
     )):
         loads[name] = pltpu.make_async_copy(source, target, local_sem.at[at])
         loads[name].start()
 
+    leave[...] = one_hot(leave_map[...], HALO)
     loads["cotangent"].wait()
     stacked[CELLS : CELLS + GROUPS, :] = cotangent[:, 0:WIDTH]
     stacked[CELLS + GROUPS :, :] = cotangent[:, WIDTH:]
     loads["tokens"].wait()
-    loads["leave"].wait()
     halo_send[...] = dot(leave[...], stacked[...]).astype(BF16)
 
     pl.semaphore_wait(barrier, len(partners))
@@ -170,7 +182,7 @@
     head_of_lane = lax.div(lax.broadcasted_iota(jnp.int32, (64, WIDTH), 1), 32)
     for h in range(HEADS):
         heads[h * 64 : (h + 1) * 64, :] = jnp.where(head_of_lane == h, 1.0, 0.0).astype(BF16)
-    loads["enter"].wait()
+    enter[...] = one_hot(enter_map[...], ROWS)
     loads["w_qkv"].wait()
     loads["gain_attn"].wait()
     loads["gain_merge"].wait()
@@ -204,17 +216,23 @@
             total = jnp.where(head_of_lane == h, wide[h * 64 : (h + 1) * 64], total)
         return total
 
-    def forward(w, carry):
-        here = rows(w, 64)
+    def over_windows(body):
+        def step(i, carry):
+            for w in range(TOGETHER):
+                body(rows(i * TOGETHER + w, 64))
+            return carry
+
+        lax.fori_loop(0, 8 // TOGETHER, step, 0)
+
+    def forward(here):
         query, key, value = (qkv[here, i * WIDTH : (i + 1) * WIDTH] for i in range(3))
         scores = dot(key, spread(query), 1, 1) * FACTOR
         powers = jnp.exp(scores - jnp.max(scores, axis=0, keepdims=True))
         weights = powers * (1.0 / jnp.sum(powers, axis=0, keepdims=True))
         probs[here, :] = weights
         attended[here, :] = gather(dot(weights.astype(BF16), value, 0, 0)).astype(BF16)
-        return carry
-
-    lax.fori_loop(0, 8, forward, 0)
+
+    over_windows(forward)
     loads["w_proj"].wait()
     summed[...] = (flat[...] + dot(attended[...], w_proj[...])).astype(BF16).astype(F32)
 
@@ -250,24 +268,32 @@
     joined = jnp.stack([g.reshape(8, 8, WIDTH) for g in grads], axis=1).reshape(CELLS, WIDTH)
     d_summed[...] = joined.astype(BF16)
 
-    q_sum[:, 3 * WIDTH :] = dot(attended[...], d_summed[...], 0, 0)
+    q_sum[0, :, WIDTH:] = dot(attended[...], d_summed[...], 0, 0)
     d_attended[...] = dot(d_summed[...], w_proj[...], 1, 1).astype(BF16)
 
-    def backward(w, carry):
-        here = rows(w, 64)
+    def backward_value(here):
+        wide = spread(d_attended[here, :])
+        d_qkv[here, 2 * WIDTH :] = dot(probs[here, :].astype(BF16), wide).astype(BF16)
+
+    over_windows(backward_value)
+    q_sum[0, :, 0:WIDTH] = dot(normal[...], d_qkv[:, 2 * WIDTH :], 0, 0)
+
+    def q_start(part):
+        return send(q_sum.at[part, :, rows(other_core, WIDTH)], q_near.at[part], partner)
+
+    q_chips = [q_start(0)]
+
+    def backward(here):
         query, key, value = (qkv[here, i * WIDTH : (i + 1) * WIDTH] for i in range(3))
         weights = probs[here, :]
         wide = spread(d_attended[here, :])
         d_probs = dot(value, wide, 1, 1)
-        d_value = dot(weights.astype(BF16), wide)
         inner = jnp.sum(d_probs * weights, axis=0, keepdims=True)
         d_scores = (weights * (d_probs - inner) * FACTOR).astype(BF16)
         d_key = dot(d_scores, spread(query))
         d_query = gather(dot(d_scores, key, 0, 0))
         d_qkv[here, 0:WIDTH] = d_query.astype(BF16)
         d_qkv[here, WIDTH : 2 * WIDTH] = d_key.astype(BF16)
-        d_qkv[here, 2 * WIDTH :] = d_value.astype(BF16)
-        return carry
 
     arrive(m_cots)
     arrive(m_rows)
@@ -282,7 +308,81 @@
         return copies
 
     m_copies = [m_second(0), m_second(1)]
-    lax.fori_loop(0, 8, backward, 0)
+
+    def q_first(part):
+        q_chips[part].wait_recv()
+        q_half[part] = q_sum[part, :, rows(core, WIDTH)] + q_near[part]
+        copies = []
+        for half in (0, 1):
+            axis = orders[half][0]
+            for step in (1, 2, 3):
+                chunk = rows(half * 4 + lax.rem(coordinate[axis] + step, 4), 32)
+                target = q_in1.at[part, half, step - 1]
+                copies.append(send(q_half.at[part, chunk], target, along(axis, step)))
+        return copies
+
+    def q_tile(at):
+        return rows(lax.div(at, 2), 16), rows(lax.rem(at, 2), 128)
+
+    def q_second(part, came):
+        arrive(came)
+        copies = []
+        for half in (0, 1):
+            first, second = orders[half]
+            own = q_half[part, rows(half * 4 + coordinate[first], 32), :]
+            q_acc1[part, half] = own + q_in1[part, half, 0] + q_in1[part, half, 1] + q_in1[part, half, 2]
+            for step in (1, 2, 3):
+                chunk = q_acc1.at[(part, half) + q_tile(lax.rem(coordinate[second] + step, 4))]
+                copies.append(send(chunk, q_in2.at[part, half, step - 1], along(second, step)))
+        return copies
+
+    def q_third(part, came):
+        arrive(came)
+        for half in (0, 1):
+            own = q_acc1[(part, half) + q_tile(coordinate[orders[half][1]])]
+            total = own + q_in2[part, half, 0] + q_in2[part, half, 1] + q_in2[part, half, 2]
+            q_in3[part, z, half * 16 : (half + 1) * 16, :] = total
+        mine = q_in3.at[part, z]
+        return [send(mine, mine, along("z", step)) for step in range(1, 8)]
+
+    def q_lanes(part, at, count):
+        return rows((1 - part) * (512 // count) + core * (WIDTH // count) + at, count)
+
+    def q_fourth(part, came):
+        arrive(came)
+        total = q_in3[part, 0]
+        for i in range(1, 8):
+            total = total + q_in3[part, i]
+        copies = []
+        for half in (0, 1):
+            first, second = orders[half]
+            high, low = lax.div(coordinate[second], 2), lax.rem(coordinate[second], 2)
+            here = (rows(half * 8 + coordinate[first] * 2 + high, 16), q_lanes(part, low, 128))
+            q_out[here] = (total[half * 16 : (half + 1) * 16] * TOKEN_SCALE).astype(BF16)
+            place = q_out.at[here]
+            copies += [send(place, place, along(second, step)) for step in (1, 2, 3)]
+        return copies
+
+    def q_fifth(part, came):
+        arrive(came)
+        copies = []
+        for half in (0, 1):
+            first = orders[half][0]
+            place = q_out.at[rows(half * 4 + coordinate[first], 32), q_lanes(part, 0, WIDTH)]
+            copies += [send(place, place, along(first, step)) for step in (1, 2, 3)]
+        return copies
+
+    def q_sixth(part, came):
+        arrive(came)
+        place = q_out.at[:, q_lanes(part, 0, WIDTH)]
+        return send(place, place, partner)
+
+    last, handed = [], []
+
+    def hand(source, target):
+        copy = pltpu.make_async_copy(source, target, out_sem.at[len(handed)])
+        copy.start()
+        handed.append(copy)
 
     def m_third(half):
         second = orders[half][1]
@@ -296,23 +396,16 @@
             copies.append(send(chunk, m_in3.at[half, step - 1], along("z", step)))
         return copies
 
-    m_copies = [m_third(0), m_third(1)]
-
-    q_sum[:, 0 : 3 * WIDTH] = dot(normal[...], d_qkv[...], 0, 0)
-    q_chip = send(q_sum.at[:, rows(other_core, 512)], q_near, partner)
-    d_normal = dot(d_qkv[...], w_qkv[...], 1, 1)
-    g_sum[8:16, :] = jnp.zeros((8, WIDTH), F32)
-    g_sum[8:9, :] = jnp.sum(d_normal * hat[...], axis=0, keepdims=True)
-    g_chip = send(g_sum, g_near, partner)
-    (d_flat,) = norm_back([hat[...]], [d_normal * gain_attn[...]], inverse_a[...], WIDTH)
-    stacked[0:CELLS, :] = (d_summed[...].astype(F32) + d_flat).astype(BF16)
-    loads["back"].wait()
-    back_send[...] = dot(back[...], stacked[...]).astype(BF16)
-    halo = []
-    for kind, start, size in list(zip(KINDS, STARTS, SIZES))[1:]:
-        block = pl.ds(start, size)
-        halo.append(send(back_send.at[block], back_recv.at[block], neighbour(kind, 1)))
-    back_recv[0 : SIZES[0], :] = back_send[0 : SIZES[0], :]
+    def g_start(total, into, axis, count):
+        into[coordinate[axis]] = total
+        mine = into.at[coordinate[axis]]
+        return [send(mine, mine, along(axis, step)) for step in range(1, count)]
+
+    def g_total(into, count):
+        total = into[0]
+        for i in range(1, count):
+            total = total + into[i]
+        return total
 
     def m_place(half, x_or_y_first, x_or_y_second):
         return half * 1024 + core * 512 + x_or_y_first * 128 + x_or_y_second * 32
@@ -326,135 +419,100 @@
             total = total + m_in3[half, step]
         start = m_place(half, coordinate[first], coordinate[second]) + high * 16
         here = (pl.ds(pl.multiple_of(start, 16), 16), lane)
-        d_merge_out[here] = (total * MERGE_SCALE).astype(BF16)
-        place = d_merge_out.at[here]
+        d_merge[here] = (total * MERGE_SCALE).astype(BF16)
+        place = d_merge.at[here]
         return [send(place, place, along("z", step)) for step in range(1, 8)]
 
-    m_copies = [m_fourth(0), m_fourth(1)]
-
-    q_chip.wait_recv()
-    q_half[...] = q_sum[:, rows(core, 512)] + q_near[...]
-
-    def q_first(half):
-        axis = orders[half][0]
-        copies = []
-        for step in (1, 2, 3):
-            chunk = half * 4 + lax.rem(coordinate[axis] + step, 4)
-            copies.append(send(q_half.at[rows(chunk, 32)], q_in1.at[half, step - 1], along(axis, step)))
-        return copies
-
-    q_copies = [q_first(0), q_first(1)]
-    g_chip.wait_recv()
-
-    def g_start(total, into, axis, count):
-        into[coordinate[axis]] = total
-        mine = into.at[coordinate[axis]]
-        return [send(mine, mine, along(axis, step)) for step in range(1, count)]
-
-    def g_total(into, count):
-        total = into[0]
-        for i in range(1, count):
-            total = total + into[i]
-        return total
-
-    g_copies = g_start(g_sum[...] + g_near[...], g_in1, "x", 4)
+    def m_pass(half, came):
+        mine, theirs = (rows(half * 8 + c * 4 + came, 128) for c in (core, other_core))
+        place = d_merge.at[mine]
+        last.append((send(place, place, partner), theirs))
+        hand(place, d_merge_out.at[mine])
 
     def m_fifth(half):
         first, second = orders[half]
         arrive(m_copies[half])
         start = m_place(half, coordinate[first], coordinate[second])
-        place = d_merge_out.at[pl.ds(pl.multiple_of(start, 32), 32)]
-        return [send(place, place, along(second, step)) for step in (1, 2, 3)]
-
-    m_copies = [m_fifth(0), m_fifth(1)]
-
-    def q_second(half):
-        first, second = orders[half]
-        arrive(q_copies[half])
-        own = q_half[rows(half * 4 + coordinate[first], 32), :]
-        q_acc1[half] = own + q_in1[half, 0] + q_in1[half, 1] + q_in1[half, 2]
-        copies = []
-        for step in (1, 2, 3):
-            lane = rows(lax.rem(coordinate[second] + step, 4), 128)
-            copies.append(send(q_acc1.at[half, :, lane], q_in2.at[half, step - 1], along(second, step)))
-        return copies
-
-    q_copies = [q_second(0), q_second(1)]
-    arrive(g_copies)
-    g_copies = g_start(g_total(g_in1, 4), g_in2, "y", 4)
+        place = d_merge.at[pl.ds(pl.multiple_of(start, 32), 32)]
+        return [send(place, place, along(second, step)) for step in (1, 3, 2)]
 
     def m_sixth(half):
         first = orders[half][0]
         arrive(m_copies[half])
-        place = d_merge_out.at[rows(half * 8 + core * 4 + coordinate[first], 128)]
-        last.append(send(place, place, partner))
-        return [send(place, place, along(first, step)) for step in (1, 3, 2)]
-
-    last = []
-    m_copies = [m_sixth(0), m_sixth(1)]
-
-    def q_third(half):
-        second = orders[half][1]
-        arrive(q_copies[half])
-        own = q_acc1[half, :, rows(coordinate[second], 128)]
-        q_acc2[half] = own + q_in2[half, 0] + q_in2[half, 1] + q_in2[half, 2]
-        q_in3[half, z] = q_acc2[half]
-        return [send(q_acc2.at[half], q_in3.at[half, z], along("z", step)) for step in range(1, 8)]
-
-    q_copies = [q_third(0), q_third(1)]
+        place = d_merge.at[rows(half * 8 + core * 4 + coordinate[first], 128)]
+        copies = [send(place, place, along(first, step)) for step in (1, 3, 2)]
+        m_pass(half, coordinate[first])
+        return copies
+
+    early = q_first(0)
+    over_windows(backward)
+    m_copies = [m_third(0), m_third(1)]
+    q_sum[1] = dot(normal[...], d_qkv[:, 0 : 2 * WIDTH], 0, 0)
+    q_chips.append(q_start(1))
+    d_normal = dot(d_qkv[...], w_qkv[...], 1, 1)
+    g_sum[8:16, :] = jnp.zeros((8, WIDTH), F32)
+    g_sum[8:9, :] = jnp.sum(d_normal * hat[...], axis=0, keepdims=True)
+    g_chip = send(g_sum, g_near, partner)
+    late = q_first(1)
+    (d_flat,) = norm_back([hat[...]], [d_normal * gain_attn[...]], inverse_a[...], WIDTH)
+    stacked[0:CELLS, :] = (d_summed[...].astype(F32) + d_flat).astype(BF16)
+    back[...] = one_hot(back_map[...], HALO)
+    back_send[...] = dot(back[...], stacked[...]).astype(BF16)
+    halo = []
+    for kind, start, size in list(zip(KINDS, STARTS, SIZES))[1:]:
+        block = pl.ds(start, size)
+        halo.append(send(back_send.at[block], back_recv.at[block], neighbour(kind, 1)))
+    back_recv[0 : SIZES[0], :] = back_send[0 : SIZES[0], :]
+    early = q_second(0, early)
+    g_chip.wait_recv()
+    g_copies = g_start(g_sum[...] + g_near[...], g_in1, "x", 4)
+    home[...] = one_hot(home_map[...], ROWS)
+
+    m_copies = [m_fourth(0), m_fourth(1)]
+    late = q_second(1, late)
+    early = q_third(0, early)
+    arrive(g_copies)
+    g_copies = g_start(g_total(g_in1, 4), g_in2, "y", 4)
+
+    arrive(halo)
+    placed = dot(home[...], back_recv[...]).astype(BF16)
+    d_tokens[...] = placed[0:CELLS]
+    merged[:, 0:WIDTH] = placed[CELLS : CELLS + GROUPS]
+    merged[:, WIDTH:] = placed[CELLS + GROUPS :]
+    hand(d_tokens, d_tokens_out)
+    hand(merged, merged_out)
+    late = q_third(1, late)
+    m_copies = [m_fifth(0), m_fifth(1)]
     arrive(g_copies)
     g_copies = g_start(g_total(g_in2, 4), g_in3, "z", 8)
-
-    loads["home"].wait()
-    arrive(halo)
-    placed = dot(home[...], back_recv[...]).astype(BF16)
-    d_tokens_out[...] = placed[0:CELLS]
-    merged_out[:, 0:WIDTH] = placed[CELLS : CELLS + GROUPS]
-    merged_out[:, WIDTH:] = placed[CELLS + GROUPS :]
-
-    def q_place(half, first_at):
-        return half * 128 + first_at * 32
-
-    def q_fifth(half):
-        first, second = orders[half]
-        arrive(q_copies[half])
-        total = q_in3[half, 0]
-        for i in range(1, 8):
-            total = total + q_in3[half, i]
-        start = pl.multiple_of(q_place(half, coordinate[first]), 32)
-        here = (pl.ds(start, 32), rows(core * 4 + coordinate[second], 128))
-        q_out[here] = (total * TOKEN_SCALE).astype(BF16)
-        place = q_out.at[here]
-        return [send(place, place, along(second, step)) for step in (1, 2, 3)]
-
-    q_copies = [q_fifth(0), q_fifth(1)]
-    for at, step in enumerate((1, 3, 2)):
-        for half in (0, 1):
-            arrive([m_copies[half][at]])
-            came = lax.rem(coordinate[orders[half][0]] + 4 - step, 4)
-            place = d_merge_out.at[rows(half * 8 + core * 4 + came, 128)]
-            last.append(send(place, place, partner))
-
-    def q_sixth(half):
-        first = orders[half][0]
-        arrive(q_copies[half])
-        start = pl.multiple_of(q_place(half, coordinate[first]), 32)
-        place = q_out.at[pl.ds(start, 32), rows(core, 512)]
-        return [send(place, place, along(first, step)) for step in (1, 2, 3)]
-
-    q_copies = [q_sixth(0), q_sixth(1)]
+    early = q_fourth(0, early)
+    m_copies = [m_sixth(0), m_sixth(1)]
+    late = q_fourth(1, late)
+    early = q_fifth(0, early)
     arrive(g_copies)
     total = g_total(g_in3, 8)
     for o in range(8):
-        d_gain_merge_out[:, o * WIDTH : (o + 1) * WIDTH] = total[o : o + 1] * MERGE_SCALE
-    d_gain_attn_out[...] = total[8:9] * TOKEN_SCALE
-    arrive(q_copies[0])
-    arrive(q_copies[1])
-    place = q_out.at[:, rows(core, 512)]
-    last.append(send(place, place, partner))
-    arrive(last)
-    d_qkv_out[...] = q_out[:, 0 : 3 * WIDTH]
-    d_proj_out[...] = q_out[:, 3 * WIDTH :]
+        d_gain_merge[:, o * WIDTH : (o + 1) * WIDTH] = total[o : o + 1] * MERGE_SCALE
+    d_gain_attn[...] = total[8:9] * TOKEN_SCALE
+    hand(d_gain_merge, d_gain_merge_out)
+    hand(d_gain_attn, d_gain_attn_out)
+    late = q_fifth(1, late)
+    early = q_sixth(0, early)
+    for at, step in enumerate((1, 3, 2)):
+        for half in (0, 1):
+            arrive([m_copies[half][at]])
+            m_pass(half, lax.rem(coordinate[orders[half][0]] + 4 - step, 4))
+    late = q_sixth(1, late)
+    arrive([early])
+    hand(q_out.at[:, pl.ds(2 * WIDTH, WIDTH)], d_qkv_out.at[:, pl.ds(2 * WIDTH, WIDTH)])
+    hand(q_out.at[:, pl.ds(3 * WIDTH, WIDTH)], d_proj_out)
+    for copy, theirs in last:
+        arrive([copy])
+        hand(d_merge.at[theirs], d_merge_out.at[theirs])
+    arrive([late])
+    hand(q_out.at[:, pl.ds(0, 2 * WIDTH)], d_qkv_out.at[:, pl.ds(0, 2 * WIDTH)])
+    for copy in handed:
+        copy.wait()
     for copy in started:
         copy.wait_send()
 
@@ -492,8 +550,8 @@
             jax.ShapeDtypeStruct((1, 8 * WIDTH), F32),
             jax.ShapeDtypeStruct((8 * WIDTH, 512), BF16),
         ),
-        in_specs=[hbm] * 11,
-        out_specs=[vmem] * 7,
+        in_specs=[hbm] * 7 + [vmem] * 4,
+        out_specs=[hbm] * 7,
         scratch_shapes=[
             pltpu.VMEM((GROUPS, 512), BF16),
             pltpu.VMEM((1, WIDTH), F32),
@@ -505,7 +563,7 @@
             pltpu.VMEM((ROWS, HALO), BF16),
             pltpu.VMEM((HALO, ROWS), BF16),
             pltpu.VMEM((ROWS, HALO), BF16),
-            pltpu.SemaphoreType.DMA((11,)),
+            pltpu.SemaphoreType.DMA((7,)),
             pltpu.VMEM((ROWS, WIDTH), BF16),
             pltpu.VMEM((HALO, WIDTH), BF16),
             pltpu.VMEM((HALO, WIDTH), BF16),
@@ -532,13 +590,12 @@
             pltpu.VMEM((2, 3, 32, 512), F32),
             pltpu.VMEM((2, 32, 512), F32),
             pltpu.VMEM((2, 7, 16, 128), F32),
-            pltpu.VMEM((WIDTH, 1024), F32),
-            pltpu.VMEM((WIDTH, 512), F32),
-            pltpu.VMEM((WIDTH, 512), F32),
-            pltpu.VMEM((2, 3, 32, 512), F32),
-            pltpu.VMEM((2, 32, 512), F32),
-            pltpu.VMEM((2, 3, 32, 128), F32),
-            pltpu.VMEM((2, 32, 128), F32),
+            pltpu.VMEM((2, WIDTH, 512), F32),
+            pltpu.VMEM((2, WIDTH, WIDTH), F32),
+            pltpu.VMEM((2, WIDTH, WIDTH), F32),
+            pltpu.VMEM((2, 2, 3, 32, WIDTH), F32),
+            pltpu.VMEM((2, 2, 32, WIDTH), F32),
+            pltpu.VMEM((2, 2, 3, 16, 128), F32),
             pltpu.VMEM((2, 8, 32, 128), F32),
             pltpu.VMEM((WIDTH, 1024), BF16),
             pltpu.VMEM((16, WIDTH), F32),
@@ -546,6 +603,12 @@
             pltpu.VMEM((4, 16, WIDTH), F32),
             pltpu.VMEM((4, 16, WIDTH), F32),
             pltpu.VMEM((8, 16, WIDTH), F32),
+            pltpu.VMEM((GROUPS, 512), BF16),
+            pltpu.VMEM((CELLS, WIDTH), BF16),
+            pltpu.VMEM((1, WIDTH), F32),
+            pltpu.VMEM((1, 8 * WIDTH), F32),
+            pltpu.VMEM((8 * WIDTH, 512), BF16),
+            pltpu.SemaphoreType.DMA((32,)),
             pltpu.SemaphoreType.DMA((copies,)),
             pltpu.SemaphoreType.DMA((copies,)),
         ],
@@ -576,8 +639,7 @@
 
 
 def solution(mesh):
-    leave, enter = orderings()
-    constants = [jnp.asarray(m, BF16) for m in (leave, enter, enter.T, leave.T)]
+    constants = [jnp.asarray(m).reshape(1, -1) for m in orderings()]
     box, whole = P("gx", "gy", "gz", None), P()
     return jax.shard_map(
         functools.partial(local, *constants),

time: 75.9 us -> 73.3 us (0.966)
  Pallas kernels: 75.2 us -> 72.5 us
    pallas_call x1, Pallas kernels: 72.4 us -> 69.7 us  [local(): pl.pallas_call(kernel, out_shape=(jax.ShapeDtypeStruct((GROUPS, 512), BF1...]
where the time goes in v3:
time: 73.3 us; the launch traced here: 73.2 us
  Pallas kernels  72.5 us (99%)
    pallas_call x1, Pallas kernels, local(): pl.pallas_call(kernel, out_shape=(jax.ShapeDtypeStruct((GROUPS, 512), BF1...  69.7 us
    pallas_call x1, Pallas kernels, local(): pl.pallas_call(hand_out, out_shape=[jax.ShapeDtypeStruct(h.shape, h.dtype...  2.82 us

profile of v3, /device:TPU:1, one launch (start us, length us, event | category | flops | bytes accessed | tf_op | source)
XLA Modules:
  0.0 73.2 jit_solution(12673914238205342294)
XLA Ops:
  0.6 69.7 %window_step.1 = (bf16[64,512]{1,0:T(8,128)(2,1)}, bf16[512,256]{1,0:T(8,128)(2,1)}, f32[1,256]{1,0:T(1,128)}, bf16[256,768]{1,0:T(8,128)(2,1)}, bf16[256,256]{1...) custom-call(bf16[512,256]{1,0:T(8,128)(2,1)} %bitcast.8, bf16[64,512]{1,0:T(8,128)(2,1)} %bitcast.10, ...), custom_call_target="tpu_custom_call" | custom-call | flops 4000000000 | bytes 12000000 | tf_op jit(solution)/shard_map/window_step/pallas_call | solution.py:542
  70.3 2.8 %hand_out.1 = (bf16[64,512]{1,0:T(8,128)(2,1)}, bf16[512,256]{1,0:T(8,128)(2,1)}, f32[1,256]{1,0:T(1,128)}, bf16[256,768]{1,0:T(8,128)(2,1)}, bf16[256,256]{1,0:...) custom-call(bf16[64,512]{1,0:T(8,128)(2,1)} %get-tuple-element.21.refs_0_, ...), custom_call_target="tpu_custom_call" | custom-call | tf_op jit(solution)/shard_map/hand_out/pallas_call | solution.py:625

commit v4 on v3

--- a/solution.py
+++ b/solution.py
@@ -16,7 +16,9 @@
 ROWS = CELLS + 2 * GROUPS
 FACTOR = 32 ** -0.5
 EPSILON = 1e-05
-TOGETHER = 2
+TOGETHER = 8
+COPIES = 171
+SENDING = 64
 TOKENS = 131072
 TOKEN_SCALE = float(TOKENS) ** (-0.5)
 MERGE_SCALE = float(TOKENS // 8) ** (-0.5)
@@ -95,7 +97,7 @@
     flat, hat, normal, inverse_a, qkv, probs, attended, summed, d_summed, d_attended, d_qkv, heads,
     cot, nm, hat_m, m_nm, m_cot, m_acc1, m_in2, m_acc2, m_in3,
     q_sum, q_near, q_half, q_in1, q_acc1, q_in2, q_in3, q_out,
-    g_sum, g_near, g_in1, g_in2, g_in3,
+    g_sum, g_near, g_in1, g_in2, g_in3, g_all,
     merged, d_tokens, d_gain_attn, d_gain_merge, d_merge, out_sem,
     send_sem, recv_sem,
 ):
@@ -131,8 +133,10 @@
 
     def send(source, target, to):
         at = len(started)
+        if at >= SENDING:
+            started[at - SENDING].wait_send()
         copy = pltpu.make_async_remote_copy(
-            src_ref=source, dst_ref=target, send_sem=send_sem.at[at], recv_sem=recv_sem.at[at],
+            src_ref=source, dst_ref=target, send_sem=send_sem.at[at % SENDING], recv_sem=recv_sem.at[at],
             device_id=to, device_id_type=MESH,
         )
         copy.start()
@@ -148,10 +152,9 @@
 
     barrier = pltpu.get_barrier_semaphore()
     partners = [neighbour(kind, sign) for kind in KINDS[1:] for sign in (-1, 1)]
-    partners += [partner]
     partners += [along(axis, step) for axis in "xy" for step in (1, 2, 3)]
     partners += [along(axis, step, other_core) for axis in "xy" for step in (1, 2, 3)]
-    partners += [along("z", step) for step in range(1, 8)]
+    partners += [along("z", step) for step in range(2, 7)]
     for there in partners:
         pl.semaphore_signal(barrier, inc=1, device_id=there, device_id_type=MESH)
 
@@ -192,15 +195,15 @@
     for t in range(2):
         part = dot(enter[CELLS + t * GROUPS : CELLS + (t + 1) * GROUPS, :], halo_recv[...])
         cot[:, t * WIDTH : (t + 1) * WIDTH] = part.astype(BF16)
-    members = [(step, flip) for step in range(4) for flip in (0, 1)]
+    members = [(step, flip) for flip in (0, 1) for step in range(4)]
     orders = (("x", "y"), ("y", "x"))
     m_cot[0, 0:GROUPS, :] = cot[...]
     m_cot[1, 0:GROUPS, :] = cot[...]
     m_cots = []
-    for at, (step, flip) in list(enumerate(members))[1:]:
-        for half in (0, 1):
-            there = along(orders[half][0], step, (core, other_core)[flip])
-            m_cots.append(send(cot, m_cot.at[half, pl.ds(at * GROUPS, GROUPS)], there))
+    for step in (1, 2, 3):
+        for half in (0, 1):
+            target = m_cot.at[half, pl.ds(step * GROUPS, GROUPS)]
+            m_cots.append(send(cot, target, along(orders[half][0], step)))
     (centred,), inverse = norm_parts([flat[...]], WIDTH)
     inverse_a[...] = inverse
     hat[...] = centred * inverse
@@ -268,6 +271,12 @@
     joined = jnp.stack([g.reshape(8, 8, WIDTH) for g in grads], axis=1).reshape(CELLS, WIDTH)
     d_summed[...] = joined.astype(BF16)
 
+    arrive(m_cots)
+    m_pairs = []
+    for half in (0, 1):
+        source = m_cot.at[half, pl.ds(0, 4 * GROUPS)]
+        m_pairs.append(send(source, m_cot.at[half, pl.ds(4 * GROUPS, 4 * GROUPS)], partner))
+
     q_sum[0, :, WIDTH:] = dot(attended[...], d_summed[...], 0, 0)
     d_attended[...] = dot(d_summed[...], w_proj[...], 1, 1).astype(BF16)
 
@@ -295,7 +304,7 @@
         d_qkv[here, 0:WIDTH] = d_query.astype(BF16)
         d_qkv[here, WIDTH : 2 * WIDTH] = d_key.astype(BF16)
 
-    arrive(m_cots)
+    arrive(m_pairs)
     arrive(m_rows)
 
     def m_second(half):
@@ -446,13 +455,12 @@
 
     early = q_first(0)
     over_windows(backward)
-    m_copies = [m_third(0), m_third(1)]
     q_sum[1] = dot(normal[...], d_qkv[:, 0 : 2 * WIDTH], 0, 0)
     q_chips.append(q_start(1))
     d_normal = dot(d_qkv[...], w_qkv[...], 1, 1)
     g_sum[8:16, :] = jnp.zeros((8, WIDTH), F32)
     g_sum[8:9, :] = jnp.sum(d_normal * hat[...], axis=0, keepdims=True)
-    g_chip = send(g_sum, g_near, partner)
+    g_chip = send(g_sum.at[:, rows(other_core, 128)], g_near, partner)
     late = q_first(1)
     (d_flat,) = norm_back([hat[...]], [d_normal * gain_attn[...]], inverse_a[...], WIDTH)
     stacked[0:CELLS, :] = (d_summed[...].astype(F32) + d_flat).astype(BF16)
@@ -464,8 +472,9 @@
         halo.append(send(back_send.at[block], back_recv.at[block], neighbour(kind, 1)))
     back_recv[0 : SIZES[0], :] = back_send[0 : SIZES[0], :]
     early = q_second(0, early)
+    m_copies = [m_third(0), m_third(1)]
     g_chip.wait_recv()
-    g_copies = g_start(g_sum[...] + g_near[...], g_in1, "x", 4)
+    g_copies = g_start(g_sum[:, rows(core, 128)] + g_near[...], g_in1, "x", 4)
     home[...] = one_hot(home_map[...], ROWS)
 
     m_copies = [m_fourth(0), m_fourth(1)]
@@ -490,14 +499,18 @@
     late = q_fourth(1, late)
     early = q_fifth(0, early)
     arrive(g_copies)
-    total = g_total(g_in3, 8)
+    g_all[:, rows(core, 128)] = g_total(g_in3, 8)
+    g_mine = g_all.at[:, rows(core, 128)]
+    g_last = send(g_mine, g_mine, partner)
+    late = q_fifth(1, late)
+    early = q_sixth(0, early)
+    g_last.wait_recv()
+    total = g_all[...]
     for o in range(8):
         d_gain_merge[:, o * WIDTH : (o + 1) * WIDTH] = total[o : o + 1] * MERGE_SCALE
     d_gain_attn[...] = total[8:9] * TOKEN_SCALE
     hand(d_gain_merge, d_gain_merge_out)
     hand(d_gain_attn, d_gain_attn_out)
-    late = q_fifth(1, late)
-    early = q_sixth(0, early)
     for at, step in enumerate((1, 3, 2)):
         for half in (0, 1):
             arrive([m_copies[half][at]])
@@ -513,7 +526,7 @@
     hand(q_out.at[:, pl.ds(0, 2 * WIDTH)], d_qkv_out.at[:, pl.ds(0, 2 * WIDTH)])
     for copy in handed:
         copy.wait()
-    for copy in started:
+    for copy in started[-SENDING:]:
         copy.wait_send()
 
 
@@ -538,7 +551,6 @@
 
 def local(leave, enter, back, home, tokens, cotangent, gain_attn, w_qkv, w_proj, gain_merge, w_merge):
     vmem, hbm = pl.BlockSpec(memory_space=pltpu.VMEM), pl.BlockSpec(memory_space=pltpu.HBM)
-    copies = 200
     held = pl.pallas_call(
         kernel,
         out_shape=(
@@ -599,18 +611,19 @@
             pltpu.VMEM((2, 8, 32, 128), F32),
             pltpu.VMEM((WIDTH, 1024), BF16),
             pltpu.VMEM((16, WIDTH), F32),
+            pltpu.VMEM((16, 128), F32),
+            pltpu.VMEM((4, 16, 128), F32),
+            pltpu.VMEM((4, 16, 128), F32),
+            pltpu.VMEM((8, 16, 128), F32),
             pltpu.VMEM((16, WIDTH), F32),
-            pltpu.VMEM((4, 16, WIDTH), F32),
-            pltpu.VMEM((4, 16, WIDTH), F32),
-            pltpu.VMEM((8, 16, WIDTH), F32),
             pltpu.VMEM((GROUPS, 512), BF16),
             pltpu.VMEM((CELLS, WIDTH), BF16),
             pltpu.VMEM((1, WIDTH), F32),
             pltpu.VMEM((1, 8 * WIDTH), F32),
             pltpu.VMEM((8 * WIDTH, 512), BF16),
-            pltpu.SemaphoreType.DMA((32,)),
-            pltpu.SemaphoreType.DMA((copies,)),
-            pltpu.SemaphoreType.DMA((copies,)),
+            pltpu.SemaphoreType.DMA((23,)),
+            pltpu.SemaphoreType.DMA((SENDING,)),
+            pltpu.SemaphoreType.DMA((COPIES,)),
         ],
         compiler_params=pltpu.CompilerParams(
             collective_id=0, has_side_effects=True, vmem_limit_bytes=60 * 1024 * 1024

time: 73.3 us -> 67.3 us (0.918)
  Pallas kernels: 72.5 us -> 66.5 us
    pallas_call x1, Pallas kernels: 69.7 us -> 63.6 us  [local(): pl.pallas_call(kernel, out_shape=(jax.ShapeDtypeStruct((GROUPS, 512), BF1...]
where the time goes in v4:
time: 67.3 us; the launch traced here: 67.1 us
  Pallas kernels  66.5 us (99%)
    pallas_call x1, Pallas kernels, local(): pl.pallas_call(kernel, out_shape=(jax.ShapeDtypeStruct((GROUPS, 512), BF1...  63.6 us
    pallas_call x1, Pallas kernels, local(): pl.pallas_call(hand_out, out_shape=[jax.ShapeDtypeStruct(h.shape, h.dtype...  2.82 us

profile of v4, /device:TPU:1, one launch (start us, length us, event | category | flops | bytes accessed | tf_op | source)
XLA Modules:
  0.0 67.1 jit_solution(5353518100930011376)
XLA Ops:
  0.6 63.6 %window_step.1 = (bf16[64,512]{1,0:T(8,128)(2,1)}, bf16[512,256]{1,0:T(8,128)(2,1)}, f32[1,256]{1,0:T(1,128)}, bf16[256,768]{1,0:T(8,128)(2,1)}, bf16[256,256]{1...) custom-call(bf16[512,256]{1,0:T(8,128)(2,1)} %bitcast.8, bf16[64,512]{1,0:T(8,128)(2,1)} %bitcast.10, ...), custom_call_target="tpu_custom_call" | custom-call | flops 4000000000 | bytes 12000000 | tf_op jit(solution)/shard_map/window_step/pallas_call | solution.py:554
  64.3 2.8 %hand_out.1 = (bf16[64,512]{1,0:T(8,128)(2,1)}, bf16[512,256]{1,0:T(8,128)(2,1)}, f32[1,256]{1,0:T(1,128)}, bf16[256,768]{1,0:T(8,128)(2,1)}, bf16[256,256]{1,0:...) custom-call(bf16[64,512]{1,0:T(8,128)(2,1)} %get-tuple-element.21.refs_0_, ...), custom_call_target="tpu_custom_call" | custom-call | tf_op jit(solution)/shard_map/hand_out/pallas_call | solution.py:638

commit v5 on v4

--- a/solution.py
+++ b/solution.py
@@ -18,7 +18,7 @@
 EPSILON = 1e-05
 TOGETHER = 8
 COPIES = 171
-SENDING = 64
+SENDING = 48
 TOKENS = 131072
 TOKEN_SCALE = float(TOKENS) ** (-0.5)
 MERGE_SCALE = float(TOKENS // 8) ** (-0.5)
@@ -191,7 +191,6 @@
     loads["gain_merge"].wait()
     arrive(halo)
 
-    flat[...] = dot(enter[0:CELLS, :], halo_recv[...])
     for t in range(2):
         part = dot(enter[CELLS + t * GROUPS : CELLS + (t + 1) * GROUPS, :], halo_recv[...])
         cot[:, t * WIDTH : (t + 1) * WIDTH] = part.astype(BF16)
@@ -204,6 +203,7 @@
         for half in (0, 1):
             target = m_cot.at[half, pl.ds(step * GROUPS, GROUPS)]
             m_cots.append(send(cot, target, along(orders[half][0], step)))
+    flat[...] = dot(enter[0:CELLS, :], halo_recv[...])
     (centred,), inverse = norm_parts([flat[...]], WIDTH)
     inverse_a[...] = inverse
     hat[...] = centred * inverse
@@ -271,12 +271,6 @@
     joined = jnp.stack([g.reshape(8, 8, WIDTH) for g in grads], axis=1).reshape(CELLS, WIDTH)
     d_summed[...] = joined.astype(BF16)
 
-    arrive(m_cots)
-    m_pairs = []
-    for half in (0, 1):
-        source = m_cot.at[half, pl.ds(0, 4 * GROUPS)]
-        m_pairs.append(send(source, m_cot.at[half, pl.ds(4 * GROUPS, 4 * GROUPS)], partner))
-
     q_sum[0, :, WIDTH:] = dot(attended[...], d_summed[...], 0, 0)
     d_attended[...] = dot(d_summed[...], w_proj[...], 1, 1).astype(BF16)
 
@@ -304,9 +298,6 @@
         d_qkv[here, 0:WIDTH] = d_query.astype(BF16)
         d_qkv[here, WIDTH : 2 * WIDTH] = d_key.astype(BF16)
 
-    arrive(m_pairs)
-    arrive(m_rows)
-
     def m_second(half):
         second = orders[half][1]
         m_acc1[half] = dot(m_nm[half], m_cot[half], 0, 0)
@@ -316,7 +307,6 @@
             copies.append(send(m_acc1.at[half, chunk], m_in2.at[half, step - 1], along(second, step)))
         return copies
 
-    m_copies = [m_second(0), m_second(1)]
 
     def q_first(part):
         q_chips[part].wait_recv()
@@ -453,7 +443,15 @@
         m_pass(half, coordinate[first])
         return copies
 
+    arrive(m_cots)
+    m_pairs = []
+    for half in (0, 1):
+        source = m_cot.at[half, pl.ds(0, 4 * GROUPS)]
+        m_pairs.append(send(source, m_cot.at[half, pl.ds(4 * GROUPS, 4 * GROUPS)], partner))
     early = q_first(0)
+    arrive(m_pairs)
+    arrive(m_rows)
+    m_copies = [m_second(0), m_second(1)]
     over_windows(backward)
     q_sum[1] = dot(normal[...], d_qkv[:, 0 : 2 * WIDTH], 0, 0)
     q_chips.append(q_start(1))
@@ -462,6 +460,8 @@
     g_sum[8:9, :] = jnp.sum(d_normal * hat[...], axis=0, keepdims=True)
     g_chip = send(g_sum.at[:, rows(other_core, 128)], g_near, partner)
     late = q_first(1)
+    g_chip.wait_recv()
+    g_copies = g_start(g_sum[:, rows(core, 128)] + g_near[...], g_in1, "x", 4)
     (d_flat,) = norm_back([hat[...]], [d_normal * gain_attn[...]], inverse_a[...], WIDTH)
     stacked[0:CELLS, :] = (d_summed[...].astype(F32) + d_flat).astype(BF16)
     back[...] = one_hot(back_map[...], HALO)
@@ -471,17 +471,13 @@
         block = pl.ds(start, size)
         halo.append(send(back_send.at[block], back_recv.at[block], neighbour(kind, 1)))
     back_recv[0 : SIZES[0], :] = back_send[0 : SIZES[0], :]
+    m_copies = [m_third(0), m_third(1)]
     early = q_second(0, early)
-    m_copies = [m_third(0), m_third(1)]
-    g_chip.wait_recv()
-    g_copies = g_start(g_sum[:, rows(core, 128)] + g_near[...], g_in1, "x", 4)
     home[...] = one_hot(home_map[...], ROWS)
-
-    m_copies = [m_fourth(0), m_fourth(1)]
+    arrive(g_copies)
+    g_copies = g_start(g_total(g_in1, 4), g_in2, "y", 4)
     late = q_second(1, late)
     early = q_third(0, early)
-    arrive(g_copies)
-    g_copies = g_start(g_total(g_in1, 4), g_in2, "y", 4)
 
     arrive(halo)
     placed = dot(home[...], back_recv[...]).astype(BF16)
@@ -490,19 +486,21 @@
     merged[:, WIDTH:] = placed[CELLS + GROUPS :]
     hand(d_tokens, d_tokens_out)
     hand(merged, merged_out)
+
+    m_copies = [m_fourth(0), m_fourth(1)]
     late = q_third(1, late)
-    m_copies = [m_fifth(0), m_fifth(1)]
     arrive(g_copies)
     g_copies = g_start(g_total(g_in2, 4), g_in3, "z", 8)
     early = q_fourth(0, early)
-    m_copies = [m_sixth(0), m_sixth(1)]
+    m_copies = [m_fifth(0), m_fifth(1)]
     late = q_fourth(1, late)
     early = q_fifth(0, early)
+    m_copies = [m_sixth(0), m_sixth(1)]
+    late = q_fifth(1, late)
     arrive(g_copies)
     g_all[:, rows(core, 128)] = g_total(g_in3, 8)
     g_mine = g_all.at[:, rows(core, 128)]
     g_last = send(g_mine, g_mine, partner)
-    late = q_fifth(1, late)
     early = q_sixth(0, early)
     g_last.wait_recv()
     total = g_all[...]

time: 67.3 us -> 67.7 us (level)
  no operation moved by 1% of the time
where the time goes in v5:
time: 67.7 us; the launch traced here: 67.6 us
  Pallas kernels  66.9 us (99%)
    pallas_call x1, Pallas kernels, local(): pl.pallas_call(kernel, out_shape=(jax.ShapeDtypeStruct((GROUPS, 512), BF1...  64.1 us
    pallas_call x1, Pallas kernels, local(): pl.pallas_call(hand_out, out_shape=[jax.ShapeDtypeStruct(h.shape, h.dtype...  2.82 us

profile of v5, /device:TPU:1, one launch (start us, length us, event | category | flops | bytes accessed | tf_op | source)
XLA Modules:
  0.0 67.6 jit_solution(7800982997535139739)
XLA Ops:
  0.6 64.1 %window_step.1 = (bf16[64,512]{1,0:T(8,128)(2,1)}, bf16[512,256]{1,0:T(8,128)(2,1)}, f32[1,256]{1,0:T(1,128)}, bf16[256,768]{1,0:T(8,128)(2,1)}, bf16[256,256]{1...) custom-call(bf16[512,256]{1,0:T(8,128)(2,1)} %bitcast.8, bf16[64,512]{1,0:T(8,128)(2,1)} %bitcast.10, ...), custom_call_target="tpu_custom_call" | custom-call | flops 4000000000 | bytes 12000000 | tf_op jit(solution)/shard_map/window_step/pallas_call | solution.py:552
  64.7 2.8 %hand_out.1 = (bf16[64,512]{1,0:T(8,128)(2,1)}, bf16[512,256]{1,0:T(8,128)(2,1)}, f32[1,256]{1,0:T(1,128)}, bf16[256,768]{1,0:T(8,128)(2,1)}, bf16[256,256]{1,0:...) custom-call(bf16[64,512]{1,0:T(8,128)(2,1)} %get-tuple-element.21.refs_0_, ...), custom_call_target="tpu_custom_call" | custom-call | tf_op jit(solution)/shard_map/hand_out/pallas_call | solution.py:636

commit v6 on v4

--- a/solution.py
+++ b/solution.py
@@ -17,8 +17,8 @@
 FACTOR = 32 ** -0.5
 EPSILON = 1e-05
 TOGETHER = 8
-COPIES = 171
-SENDING = 64
+COPIES = 164
+SENDING = 48
 TOKENS = 131072
 TOKEN_SCALE = float(TOKENS) ** (-0.5)
 MERGE_SCALE = float(TOKENS // 8) ** (-0.5)
@@ -90,9 +90,9 @@
 
 def kernel(
     tokens_hbm, cotangent_hbm, gain_attn_hbm, gain_merge_hbm, w_qkv_hbm, w_proj_hbm, w_merge_hbm,
-    leave_map, enter_map, back_map, home_map,
+    maps_hbm,
     merged_out, d_tokens_out, d_gain_attn_out, d_qkv_out, d_proj_out, d_gain_merge_out, d_merge_out,
-    cotangent, gain_attn, gain_merge, w_qkv, w_proj, w_merge, leave, enter, back, home, local_sem,
+    cotangent, gain_attn, gain_merge, w_qkv, w_proj, w_merge, leave, enter, back, home, maps, local_sem,
     stacked, halo_send, halo_recv, back_send, back_recv,
     flat, hat, normal, inverse_a, qkv, probs, attended, summed, d_summed, d_attended, d_qkv, heads,
     cot, nm, hat_m, m_nm, m_cot, m_acc1, m_in2, m_acc2, m_in3,
@@ -150,6 +150,16 @@
     def rows(at, count):
         return pl.ds(pl.multiple_of(at * count, count), count)
 
+    loads = {}
+
+    def load(name, source, target):
+        loads[name] = pltpu.make_async_copy(source, target, local_sem.at[len(loads)])
+        loads[name].start()
+
+    load("maps", maps_hbm, maps)
+    load("tokens", tokens_hbm, stacked.at[pl.ds(0, CELLS)])
+    load("cotangent", cotangent_hbm, cotangent)
+
     barrier = pltpu.get_barrier_semaphore()
     partners = [neighbour(kind, sign) for kind in KINDS[1:] for sign in (-1, 1)]
     partners += [along(axis, step) for axis in "xy" for step in (1, 2, 3)]
@@ -158,18 +168,13 @@
     for there in partners:
         pl.semaphore_signal(barrier, inc=1, device_id=there, device_id_type=MESH)
 
-    loads = {}
-    for at, (name, source, target) in enumerate((
-        ("tokens", tokens_hbm, stacked.at[pl.ds(0, CELLS)]),
-        ("cotangent", cotangent_hbm, cotangent), ("gain_attn", gain_attn_hbm, gain_attn),
-        ("gain_merge", gain_merge_hbm, gain_merge),
-        ("w_qkv", w_qkv_hbm, w_qkv),
-        ("w_proj", w_proj_hbm, w_proj), ("w_merge", w_merge_hbm, w_merge),
-    )):
-        loads[name] = pltpu.make_async_copy(source, target, local_sem.at[at])
-        loads[name].start()
-
-    leave[...] = one_hot(leave_map[...], HALO)
+    load("w_qkv", w_qkv_hbm, w_qkv)
+    load("gain_attn", gain_attn_hbm, gain_attn)
+    load("gain_merge", gain_merge_hbm, gain_merge)
+    load("w_proj", w_proj_hbm, w_proj)
+    load("w_merge", w_merge_hbm, w_merge)
+    loads["maps"].wait()
+    leave[...] = one_hot(maps[0:1, 0:ROWS], HALO)
     loads["cotangent"].wait()
     stacked[CELLS : CELLS + GROUPS, :] = cotangent[:, 0:WIDTH]
     stacked[CELLS + GROUPS :, :] = cotangent[:, WIDTH:]
@@ -185,7 +190,7 @@
     head_of_lane = lax.div(lax.broadcasted_iota(jnp.int32, (64, WIDTH), 1), 32)
     for h in range(HEADS):
         heads[h * 64 : (h + 1) * 64, :] = jnp.where(head_of_lane == h, 1.0, 0.0).astype(BF16)
-    enter[...] = one_hot(enter_map[...], ROWS)
+    enter[...] = one_hot(maps[1:2, 0:HALO], ROWS)
     loads["w_qkv"].wait()
     loads["gain_attn"].wait()
     loads["gain_merge"].wait()
@@ -393,16 +398,16 @@
         copy.start()
         handed.append(copy)
 
-    def m_third(half):
-        second = orders[half][1]
-        arrive(m_copies[half])
-        own = m_acc1[half, rows(coordinate[second], 32), :]
-        m_acc2[half] = own + m_in2[half, 0] + m_in2[half, 1] + m_in2[half, 2]
+    def m_third(came):
+        arrive(came)
+        for half in (0, 1):
+            own = m_acc1[half, rows(coordinate[orders[half][1]], 32), :]
+            m_acc2[half] = own + m_in2[half, 0] + m_in2[half, 1] + m_in2[half, 2]
         copies = []
         for step in range(1, 8):
             there = lax.rem(z + step, 8)
-            chunk = m_acc2.at[half, rows(lax.div(there, 4), 16), rows(lax.rem(there, 4), 128)]
-            copies.append(send(chunk, m_in3.at[half, step - 1], along("z", step)))
+            chunk = m_acc2.at[:, rows(lax.div(there, 4), 16), rows(lax.rem(there, 4), 128)]
+            copies.append(send(chunk, m_in3.at[step - 1], along("z", step)))
         return copies
 
     def g_start(total, into, axis, count):
@@ -421,11 +426,10 @@
 
     def m_fourth(half):
         first, second = orders[half]
-        arrive(m_copies[half])
         high, lane = lax.div(z, 4), rows(lax.rem(z, 4), 128)
         total = m_acc2[half, rows(high, 16), lane]
         for step in range(7):
-            total = total + m_in3[half, step]
+            total = total + m_in3[step, half]
         start = m_place(half, coordinate[first], coordinate[second]) + high * 16
         here = (pl.ds(pl.multiple_of(start, 16), 16), lane)
         d_merge[here] = (total * MERGE_SCALE).astype(BF16)
@@ -464,7 +468,7 @@
     late = q_first(1)
     (d_flat,) = norm_back([hat[...]], [d_normal * gain_attn[...]], inverse_a[...], WIDTH)
     stacked[0:CELLS, :] = (d_summed[...].astype(F32) + d_flat).astype(BF16)
-    back[...] = one_hot(back_map[...], HALO)
+    back[...] = one_hot(maps[2:3, 0:ROWS], HALO)
     back_send[...] = dot(back[...], stacked[...]).astype(BF16)
     halo = []
     for kind, start, size in list(zip(KINDS, STARTS, SIZES))[1:]:
@@ -472,11 +476,12 @@
         halo.append(send(back_send.at[block], back_recv.at[block], neighbour(kind, 1)))
     back_recv[0 : SIZES[0], :] = back_send[0 : SIZES[0], :]
     early = q_second(0, early)
-    m_copies = [m_third(0), m_third(1)]
+    m_copies = m_third(m_copies[0] + m_copies[1])
     g_chip.wait_recv()
     g_copies = g_start(g_sum[:, rows(core, 128)] + g_near[...], g_in1, "x", 4)
-    home[...] = one_hot(home_map[...], ROWS)
-
+    home[...] = one_hot(maps[3:4, 0:HALO], ROWS)
+
+    arrive(m_copies)
     m_copies = [m_fourth(0), m_fourth(1)]
     late = q_second(1, late)
     early = q_third(0, early)
@@ -549,8 +554,8 @@
         copy_out.wait()
 
 
-def local(leave, enter, back, home, tokens, cotangent, gain_attn, w_qkv, w_proj, gain_merge, w_merge):
-    vmem, hbm = pl.BlockSpec(memory_space=pltpu.VMEM), pl.BlockSpec(memory_space=pltpu.HBM)
+def local(maps, tokens, cotangent, gain_attn, w_qkv, w_proj, gain_merge, w_merge):
+    hbm = pl.BlockSpec(memory_space=pltpu.HBM)
     held = pl.pallas_call(
         kernel,
         out_shape=(
@@ -562,7 +567,7 @@
             jax.ShapeDtypeStruct((1, 8 * WIDTH), F32),
             jax.ShapeDtypeStruct((8 * WIDTH, 512), BF16),
         ),
-        in_specs=[hbm] * 7 + [vmem] * 4,
+        in_specs=[hbm] * 8,
         out_specs=[hbm] * 7,
         scratch_shapes=[
             pltpu.VMEM((GROUPS, 512), BF16),
@@ -575,7 +580,8 @@
             pltpu.VMEM((ROWS, HALO), BF16),
             pltpu.VMEM((HALO, ROWS), BF16),
             pltpu.VMEM((ROWS, HALO), BF16),
-            pltpu.SemaphoreType.DMA((7,)),
+            pltpu.VMEM((8, 768), jnp.int32),
+            pltpu.SemaphoreType.DMA((8,)),
             pltpu.VMEM((ROWS, WIDTH), BF16),
             pltpu.VMEM((HALO, WIDTH), BF16),
             pltpu.VMEM((HALO, WIDTH), BF16),
@@ -601,7 +607,7 @@
             pltpu.VMEM((2, 128, 512), F32),
             pltpu.VMEM((2, 3, 32, 512), F32),
             pltpu.VMEM((2, 32, 512), F32),
-            pltpu.VMEM((2, 7, 16, 128), F32),
+            pltpu.VMEM((7, 2, 16, 128), F32),
             pltpu.VMEM((2, WIDTH, 512), F32),
             pltpu.VMEM((2, WIDTH, WIDTH), F32),
             pltpu.VMEM((2, WIDTH, WIDTH), F32),
@@ -633,7 +639,7 @@
     )(
         tokens.reshape(CELLS, WIDTH), cotangent.reshape(GROUPS, 512),
         gain_attn.reshape(1, WIDTH), gain_merge.reshape(1, 8 * WIDTH),
-        w_qkv, w_proj, w_merge, leave, enter, back, home,
+        w_qkv, w_proj, w_merge, maps,
     )
     outs = pl.pallas_call(
         hand_out,
@@ -652,10 +658,12 @@
 
 
 def solution(mesh):
-    constants = [jnp.asarray(m).reshape(1, -1) for m in orderings()]
+    maps = np.full((8, 768), -1, np.int32)
+    for at, rows_of_columns in enumerate(orderings()):
+        maps[at, : len(rows_of_columns)] = rows_of_columns
     box, whole = P("gx", "gy", "gz", None), P()
     return jax.shard_map(
-        functools.partial(local, *constants),
+        functools.partial(local, jnp.asarray(maps)),
         mesh=mesh,
         in_specs=(box, box, whole, whole, whole, whole, whole),
         out_specs=(box, box, whole, whole, whole, whole, whole),

time: 67.3 us -> 67.5 us (level)
  no operation moved by 1% of the time
where the time goes in v6:
time: 67.5 us; the launch traced here: 67.3 us
  Pallas kernels  66.7 us (99%)
    pallas_call x1, Pallas kernels, local(): pl.pallas_call(kernel, out_shape=(jax.ShapeDtypeStruct((GROUPS, 512), BF1...  63.9 us
    pallas_call x1, Pallas kernels, local(): pl.pallas_call(hand_out, out_shape=[jax.ShapeDtypeStruct(h.shape, h.dtype...  2.82 us

profile of v6, /device:TPU:1, one launch (start us, length us, event | category | flops | bytes accessed | tf_op | source)
XLA Modules:
  0.0 67.3 jit_solution(1939684906309008314)
XLA Ops:
  0.6 63.9 %window_step.1 = (bf16[64,512]{1,0:T(8,128)(2,1)}, bf16[512,256]{1,0:T(8,128)(2,1)}, f32[1,256]{1,0:T(1,128)}, bf16[256,768]{1,0:T(8,128)(2,1)}, bf16[256,256]{1...) custom-call(bf16[512,256]{1,0:T(8,128)(2,1)} %bitcast.8, bf16[64,512]{1,0:T(8,128)(2,1)} %bitcast.10, ...), custom_call_target="tpu_custom_call" | custom-call | flops 4000000000 | bytes 12000000 | tf_op jit(solution)/shard_map/window_step/pallas_call | solution.py:559
  64.5 2.8 %hand_out.1 = (bf16[64,512]{1,0:T(8,128)(2,1)}, bf16[512,256]{1,0:T(8,128)(2,1)}, f32[1,256]{1,0:T(1,128)}, bf16[256,768]{1,0:T(8,128)(2,1)}, bf16[256,256]{1,0:...) custom-call(bf16[64,512]{1,0:T(8,128)(2,1)} %get-tuple-element.21.refs_0_, ...), custom_call_target="tpu_custom_call" | custom-call | tf_op jit(solution)/shard_map/hand_out/pallas_call | solution.py:644

commit v7 on v6

--- a/solution.py
+++ b/solution.py
@@ -196,7 +196,6 @@
     loads["gain_merge"].wait()
     arrive(halo)
 
-    flat[...] = dot(enter[0:CELLS, :], halo_recv[...])
     for t in range(2):
         part = dot(enter[CELLS + t * GROUPS : CELLS + (t + 1) * GROUPS, :], halo_recv[...])
         cot[:, t * WIDTH : (t + 1) * WIDTH] = part.astype(BF16)
@@ -209,6 +208,7 @@
         for half in (0, 1):
             target = m_cot.at[half, pl.ds(step * GROUPS, GROUPS)]
             m_cots.append(send(cot, target, along(orders[half][0], step)))
+    flat[...] = dot(enter[0:CELLS, :], halo_recv[...])
     (centred,), inverse = norm_parts([flat[...]], WIDTH)
     inverse_a[...] = inverse
     hat[...] = centred * inverse
@@ -276,12 +276,6 @@
     joined = jnp.stack([g.reshape(8, 8, WIDTH) for g in grads], axis=1).reshape(CELLS, WIDTH)
     d_summed[...] = joined.astype(BF16)
 
-    arrive(m_cots)
-    m_pairs = []
-    for half in (0, 1):
-        source = m_cot.at[half, pl.ds(0, 4 * GROUPS)]
-        m_pairs.append(send(source, m_cot.at[half, pl.ds(4 * GROUPS, 4 * GROUPS)], partner))
-
     q_sum[0, :, WIDTH:] = dot(attended[...], d_summed[...], 0, 0)
     d_attended[...] = dot(d_summed[...], w_proj[...], 1, 1).astype(BF16)
 
@@ -309,9 +303,6 @@
         d_qkv[here, 0:WIDTH] = d_query.astype(BF16)
         d_qkv[here, WIDTH : 2 * WIDTH] = d_key.astype(BF16)
 
-    arrive(m_pairs)
-    arrive(m_rows)
-
     def m_second(half):
         second = orders[half][1]
         m_acc1[half] = dot(m_nm[half], m_cot[half], 0, 0)
@@ -321,7 +312,6 @@
             copies.append(send(m_acc1.at[half, chunk], m_in2.at[half, step - 1], along(second, step)))
         return copies
 
-    m_copies = [m_second(0), m_second(1)]
 
     def q_first(part):
         q_chips[part].wait_recv()
@@ -457,7 +447,15 @@
         m_pass(half, coordinate[first])
         return copies
 
+    arrive(m_cots)
+    m_pairs = []
+    for half in (0, 1):
+        source = m_cot.at[half, pl.ds(0, 4 * GROUPS)]
+        m_pairs.append(send(source, m_cot.at[half, pl.ds(4 * GROUPS, 4 * GROUPS)], partner))
     early = q_first(0)
+    arrive(m_pairs)
+    arrive(m_rows)
+    m_copies = [m_second(0), m_second(1)]
     over_windows(backward)
     q_sum[1] = dot(normal[...], d_qkv[:, 0 : 2 * WIDTH], 0, 0)
     q_chips.append(q_start(1))

time: 67.5 us -> 67.3 us (level)
  no operation moved by 1% of the time
where the time goes in v7:
time: 67.3 us; the launch traced here: 67.2 us
  Pallas kernels  66.6 us (99%)
    pallas_call x1, Pallas kernels, local(): pl.pallas_call(kernel, out_shape=(jax.ShapeDtypeStruct((GROUPS, 512), BF1...  63.7 us
    pallas_call x1, Pallas kernels, local(): pl.pallas_call(hand_out, out_shape=[jax.ShapeDtypeStruct(h.shape, h.dtype...  2.82 us

profile of v7, /device:TPU:1, one launch (start us, length us, event | category | flops | bytes accessed | tf_op | source)
XLA Modules:
  0.0 67.2 jit_solution(7959441235734484198)
XLA Ops:
  0.6 63.7 %window_step.1 = (bf16[64,512]{1,0:T(8,128)(2,1)}, bf16[512,256]{1,0:T(8,128)(2,1)}, f32[1,256]{1,0:T(1,128)}, bf16[256,768]{1,0:T(8,128)(2,1)}, bf16[256,256]{1...) custom-call(bf16[512,256]{1,0:T(8,128)(2,1)} %bitcast.8, bf16[64,512]{1,0:T(8,128)(2,1)} %bitcast.10, ...), custom_call_target="tpu_custom_call" | custom-call | flops 4000000000 | bytes 12000000 | tf_op jit(solution)/shard_map/window_step/pallas_call | solution.py:557
  64.4 2.8 %hand_out.1 = (bf16[64,512]{1,0:T(8,128)(2,1)}, bf16[512,256]{1,0:T(8,128)(2,1)}, f32[1,256]{1,0:T(1,128)}, bf16[256,768]{1,0:T(8,128)(2,1)}, bf16[256,256]{1,0:...) custom-call(bf16[64,512]{1,0:T(8,128)(2,1)} %get-tuple-element.21.refs_0_, ...), custom_call_target="tpu_custom_call" | custom-call | tf_op jit(solution)/shard_map/hand_out/pallas_call | solution.py:642
